TPU v7x, 32 devices: a whole 2x2x4 slice. The times are simulated.
32 devices in a mesh: seq: 16 (over z, y, core), tp: 2 (over x).
Axes of the slice: x: 2, y: 2, z: 4, core: 2. Of those that a mesh axis runs over, the one named last changes fastest.
Arguments:
- q_proj: bfloat16 [2048, 8192], P('seq', 'tp'), may hold values from -6 to 6
- k_proj: bfloat16 [2048, 8192], P('seq', 'tp'), may hold values from -6 to 6
- v_proj: bfloat16 [2048, 8192], P('seq', 'tp'), may hold values from -6 to 6
- grad_out: bfloat16 [2048, 8192], P('seq', 'tp'), may hold values from -6 to 6
- w_first: float32 [32, 64], replicated, may hold values from -2 to 2
- w_second: float32 [64, 8192], P(None, 'tp'), may hold values from -0.75 to 0.75
- decay_rate: float32 [8192], P('tp'), may hold values from 0.02 to 64
- skip_gain: float32 [8192], P('tp'), may hold values from 0.5 to 1.5
Outputs:
- grad_q: bfloat16 [2048, 8192], P('seq', 'tp')
- grad_k: bfloat16 [2048, 8192], P('seq', 'tp')
- grad_v: bfloat16 [2048, 8192], P('seq', 'tp')
- grad_first: float32 [32, 64], replicated
- grad_second: float32 [64, 8192], P(None, 'tp')
- grad_decay: float32 [8192], P('tp')
- grad_skip: float32 [8192], P('tp')
All inputs are finite; a program needn't handle non-finite values.
Results may differ from a plain program's by a relative error of at most 0.0058.
Values may be sent and summed in bfloat16 or wider, within the bound.
No kernel may reach another device: no remote copies, remote signals or barrier semaphores. Data moves between devices by JAX's collectives and lax.ppermute only.
A program may use at most 128 MiB of HBM per device.

v0:
```python
import functools
import math

import jax
import jax.numpy as jnp
import ml_dtypes
import numpy as np
from jax import lax
from jax.experimental import pallas as pl
from jax.experimental.pallas import tpu as pltpu
from jax.sharding import PartitionSpec as P

HIGH = lax.Precision.HIGHEST
MIB = 1024 * 1024


def positional_table(length, band_count):
    positions = jnp.arange(length, dtype=jnp.int32)
    band_index = jnp.arange(band_count, dtype=jnp.int32)
    frequency = 3 * (band_index + 1) * (band_index + 1) + band_index
    phase_index = frequency[:, None] * positions[None, :] % length
    angles = phase_index.astype(jnp.float32) * (2.0 * math.pi / length)
    return jnp.concatenate([jnp.sin(angles), jnp.cos(angles)], axis=0)


@functools.lru_cache(maxsize=None)
def transform_tables(length, height):
    j = np.arange(height)
    angles = (j[:, None] * j[None, :] % height) * (2.0 * np.pi / height)
    cosine, sine = np.cos(angles), np.sin(angles)
    forward = np.concatenate(
        [np.concatenate([cosine, -sine], axis=1), np.concatenate([sine, cosine], axis=1)], axis=0
    )
    return np.stack([forward, forward.T / length]).astype(np.float32)


@functools.lru_cache(maxsize=None)
def twiddle_table(length, height):
    parts = length // height
    r = np.arange(parts)[:, None]
    j = np.arange(height)[None, :]
    angles = (j * (4 * r + 1) % (4 * length)) * (2.0 * np.pi / (4 * length))
    return np.concatenate([np.cos(angles), -np.sin(angles)], axis=1).astype(np.float32)


def turn(value, cosine, sine):
    real, imag = value
    return (real * cosine - imag * sine, real * sine + imag * cosine)


def small_fft(values, sign):
    count = len(values)
    if count == 1:
        return values
    even = small_fft(values[0::2], sign)
    odd = small_fft(values[1::2], sign)
    first, second = [], []
    for k in range(count // 2):
        real, imag = odd[k]
        if k == 0:
            pass
        elif 4 * k == count:
            real, imag = (-imag, real) if sign > 0 else (imag, -real)
        elif 8 * k == count:
            half = math.sqrt(0.5)
            if sign > 0:
                real, imag = (real - imag) * half, (real + imag) * half
            else:
                real, imag = (real + imag) * half, (imag - real) * half
        elif 8 * k == 3 * count:
            half = math.sqrt(0.5)
            if sign > 0:
                real, imag = (real + imag) * -half, (real - imag) * half
            else:
                real, imag = (imag - real) * half, (real + imag) * -half
        else:
            angle = sign * 2.0 * math.pi * k / count
            real, imag = turn((real, imag), math.cos(angle), math.sin(angle))
        base_real, base_imag = even[k]
        first.append((base_real + real, base_imag + imag))
        second.append((base_real - real, base_imag - imag))
    return first + second


def parts_forward(values):
    count = len(values)
    turned = []
    for p, value in enumerate(values):
        angle = 2.0 * math.pi * p / (4 * count)
        turned.append((value * math.cos(angle), value * -math.sin(angle)))
    return small_fft(turned, -1)


def parts_inverse(values):
    count = len(values)
    result = []
    for p, (real, imag) in enumerate(small_fft(values, 1)):
        angle = 2.0 * math.pi * p / (4 * count)
        result.append(real * math.cos(angle) - imag * math.sin(angle))
    return result


def split_bf16(value):
    high = value.astype(jnp.bfloat16)
    return high, (value - high.astype(jnp.float32)).astype(jnp.bfloat16)


def split_table(table_ref, split):
    size = table_ref.shape[1]
    for direction in range(2):
        high, low = split_bf16(table_ref[direction])
        split[direction, :size] = high
        split[direction, size : 2 * size] = high
        split[direction, 2 * size :] = low


def transform(value, split, direction):
    high, low = split_bf16(value)
    return jnp.dot(
        jnp.concatenate([high, low, high], axis=1),
        split[direction],
        preferred_element_type=jnp.float32,
    )


def spectrum_product(left, right, conjugate):
    height = left.shape[1] // 2
    left_real, left_imag = left[:, :height], left[:, height:]
    right_real, right_imag = right[:, :height], right[:, height:]
    if conjugate:
        real = left_real * right_real + left_imag * right_imag
        imag = left_real * right_imag - left_imag * right_real
    else:
        real = left_real * right_real - left_imag * right_imag
        imag = left_real * right_imag + left_imag * right_real
    return jnp.concatenate([real, imag], axis=1)


def first_chunk(load, work, twiddle_ref, index):
    parts, height = work.shape[0], work.shape[2] // 2
    row = pl.multiple_of(index * 16, 16)
    values = [load(p, row) for p in range(parts)]
    for half in (0, 8):
        rows = pl.ds(row + half, 8)
        turned = parts_forward([value[half : half + 8] for value in values])
        for r, value in enumerate(turned):
            cosine = twiddle_ref[r : r + 1, :height]
            sine = twiddle_ref[r : r + 1, height:]
            work[r, rows, :height], work[r, rows, height:] = turn(value, cosine, sine)


def last_chunk(store, work, twiddle_ref, index):
    parts, height = work.shape[0], work.shape[2] // 2
    row = pl.multiple_of(index * 16, 16)
    halves = []
    for half in (0, 8):
        rows = pl.ds(row + half, 8)
        values = []
        for r in range(parts):
            cosine = twiddle_ref[r : r + 1, :height]
            sine = twiddle_ref[r : r + 1, height:]
            value = (work[r, rows, :height], work[r, rows, height:])
            values.append(turn(value, cosine, -sine))
        halves.append(parts_inverse(values))
    for p in range(parts):
        store(p, row, jnp.concatenate([halves[0][p], halves[1][p]], axis=0))


GROUP = 4


def run_chunks(width, chunk, parts=0, block=None):
    chunks = width // 16
    per = math.gcd(chunks, GROUP)
    paired = parts * per == GROUP * chunks

    def one(index, carry):
        if paired:
            block(index * GROUP)
        for b in range(per):
            chunk(index * per + b)
        return carry

    lax.fori_loop(0, chunks // per, one, 0)
    if not paired and parts > 0:
        run_blocks(parts, block)


def run_blocks(parts, block):
    def one(index, carry):
        block(index * GROUP)
        return carry

    lax.fori_loop(0, parts // GROUP, one, 0)


def group_of(r):
    return pl.ds(pl.multiple_of(r, GROUP), GROUP)


def read_group(ref, r):
    _, width, columns = ref.shape
    return ref[group_of(r)].reshape(GROUP * width, columns)


def write_group(ref, r, value):
    ref[group_of(r)] = value.reshape((GROUP,) + ref.shape[1:])


def envelope_at(decay, start, length, height):
    position = (start + lax.broadcasted_iota(jnp.int32, (1, height), 1)).astype(jnp.float32)
    fraction = position * (1.0 / length)
    return jnp.exp(-decay * fraction), fraction


def columns_of(p, height):
    return slice(p * height, (p + 1) * height)


def filter_kernel(
    w_t_ref, hidden_ref, decay_ref, table_ref, twiddle_ref, filter_ref, spectrum_ref, work, split
):
    parts, width, height = work.shape[0], work.shape[1], work.shape[2] // 2
    length = filter_ref.shape[1]
    scale = length**-0.5
    split_table(table_ref, split)
    filter_ref[...] = jnp.dot(
        w_t_ref[...], hidden_ref[...], precision=HIGH, preferred_element_type=jnp.float32
    )

    def load(p, row):
        rows, columns = pl.ds(row, 16), columns_of(p, height)
        envelope, _ = envelope_at(decay_ref[rows, :], p * height, length, height)
        value = filter_ref[rows, columns] * envelope * scale
        filter_ref[rows, columns] = value
        return value

    def block(r):
        write_group(spectrum_ref, r, transform(read_group(work, r), split, 0))

    run_chunks(width, lambda i: first_chunk(load, work, twiddle_ref, i))
    run_blocks(parts, block)


def load_from(ref):
    def load(p, row):
        return ref[p, pl.ds(row, 16), :].astype(jnp.float32)

    return load


def store_to(ref, skip_ref, load):
    def store(p, row, value):
        value = value + skip_ref[pl.ds(row, 16), :] * load(p, row)
        ref[p, pl.ds(row, 16), :] = value.astype(jnp.bfloat16)

    return store


def conv_kernel(
    x_ref, h_any, table_ref, twiddle_ref, skip_ref, y_ref, x_any, work, spectra, h, split, sems
):
    parts, width = work.shape[0], work.shape[1]
    copy_in = pltpu.make_async_copy(h_any, h, sems.at[0])
    copy_in.start()
    split_table(table_ref, split)
    load = load_from(x_ref)

    def block(r):
        spectrum = transform(read_group(work, r), split, 0)
        write_group(spectra, r, spectrum)
        product = spectrum_product(read_group(h, r), spectrum, False)
        write_group(work, r, transform(product, split, 1))

    run_chunks(width, lambda i: first_chunk(load, work, twiddle_ref, i))
    copy_in.wait()
    run_blocks(parts, block)
    copy_out = pltpu.make_async_copy(spectra, x_any, sems.at[1])
    copy_out.start()
    store = store_to(y_ref, skip_ref, load)
    run_chunks(width, lambda i: last_chunk(store, work, twiddle_ref, i))
    copy_out.wait()


def grad_kernel(
    x_ref,
    g_ref,
    x_any,
    h_any,
    filter_any,
    table_ref,
    twiddle_ref,
    skip_ref,
    decay_ref,
    hidden_ref,
    w_ref,
    cosine_ref,
    positional_ref,
    z_ref,
    small_ref,
    first_ref,
    work,
    cross,
    h,
    raw,
    sums,
    split,
    sems,
):
    parts, height = work.shape[0], work.shape[2] // 2
    width, length = raw.shape
    hidden_count = hidden_ref.shape[0]
    scale = length**-0.5
    copies = [
        pltpu.make_async_copy(source, target, sems.at[at])
        for at, (source, target) in enumerate(((x_any, cross), (h_any, h), (filter_any, raw)))
    ]
    for copy in copies:
        copy.start()
    split_table(table_ref, split)
    load = load_from(g_ref)

    def block(r):
        spectrum = transform(read_group(work, r), split, 0)
        product = spectrum_product(read_group(h, r), spectrum, True)
        write_group(work, r, transform(product, split, 1))
        product = spectrum_product(read_group(cross, r), spectrum, True)
        write_group(cross, r, transform(product, split, 1))

    def store(p, row, value):
        rows, columns = pl.ds(row, 16), columns_of(p, height)
        envelope, fraction = envelope_at(decay_ref[rows, :], p * height, length, height)
        decay_part = value * raw[rows, columns] * fraction
        skip_part = load_from(x_ref)(p, row) * load(p, row)
        raw[rows, columns] = value * envelope * scale
        if p > 0:
            decay_part = decay_part + sums[0, rows, :]
            skip_part = skip_part + sums[1, rows, :]
        sums[0, rows, :] = decay_part
        sums[1, rows, :] = skip_part

    run_chunks(width, lambda i: first_chunk(load, work, twiddle_ref, i))
    for copy in copies:
        copy.wait()
    run_blocks(parts, block)
    store_z = store_to(z_ref, skip_ref, load)
    run_chunks(width, lambda i: last_chunk(store_z, work, twiddle_ref, i))
    run_chunks(width, lambda i: last_chunk(store, cross, twiddle_ref, i))

    def dot_pairs(left, right, along):
        def dot(one, two):
            return lax.dot_general(
                one, two, (((1,), (along,)), ((), ())), preferred_element_type=jnp.float32
            )

        return dot(left[0], right[0]) + (dot(left[0], right[1]) + dot(left[1], right[0]))

    second = jnp.zeros((hidden_count, width), jnp.float32)
    band_total = positional_ref.shape[0]
    first = jnp.zeros((band_total, hidden_count), jnp.float32)
    w_pair = split_bf16(w_ref[...])
    chunk = min(length, 512)
    for at in range(0, length, chunk):
        columns = slice(at, at + chunk)
        raw_pair = split_bf16(raw[:, columns])
        second += dot_pairs(split_bf16(hidden_ref[:, columns]), raw_pair, 1)
        hidden_part = dot_pairs(w_pair, raw_pair, 0) * cosine_ref[:, columns]
        first += dot_pairs(split_bf16(positional_ref[:, columns]), split_bf16(hidden_part), 1)

    first_ref[:band_total, :], first_ref[band_total:, :] = split_bf16(first * scale)
    small_ref[:hidden_count, :] = (second * scale).astype(jnp.bfloat16)
    place = lax.broadcasted_iota(jnp.int32, (16, width), 0)
    tail = jnp.zeros((16, width), jnp.float32)
    decay_pair = split_bf16(jnp.sum(sums[0].T, axis=0, keepdims=True) * -scale)
    skip_pair = split_bf16(jnp.sum(sums[1].T, axis=0, keepdims=True) * scale)
    for at, row in enumerate(decay_pair + skip_pair):
        tail = jnp.where(place == at, row.astype(jnp.float32), tail)
    small_ref[hidden_count:, :] = tail.astype(jnp.bfloat16)


def params():
    return pltpu.CompilerParams(vmem_limit_bytes=56 * MIB)


def estimate(flops, nbytes):
    return pl.CostEstimate(flops=flops, bytes_accessed=nbytes, transcendentals=0)


def gate_kernel(left_ref, right_ref, out_ref):
    width = out_ref.shape[1]
    for at in range(out_ref.shape[0]):
        lanes = slice(at * width, (at + 1) * width)
        left = left_ref[:, lanes].astype(jnp.float32)
        right = right_ref[:, lanes].astype(jnp.float32)
        out_ref[at] = (left * right).T.astype(jnp.bfloat16)


def gate(left, right, count):
    rows, columns = left.shape
    width = columns // count
    if width % 128 != 0:
        product = (left.astype(jnp.float32) * right.astype(jnp.float32)).astype(jnp.bfloat16)
        return product.reshape(rows, count, width).transpose(1, 2, 0)
    group = math.gcd(count, 4)
    return pl.pallas_call(
        gate_kernel,
        grid=(count // group,),
        in_specs=[pl.BlockSpec((rows, group * width), lambda i: (0, i))] * 2,
        out_specs=pl.BlockSpec((group, width, rows), lambda i: (i, 0, 0)),
        out_shape=jax.ShapeDtypeStruct((count, width, rows), jnp.bfloat16),
        compiler_params=params(),
        cost_estimate=estimate(rows * columns, rows * columns * 6),
    )(left, right)


def ungate_kernel(back_ref, *refs):
    count = len(refs) // 2
    width = back_ref.shape[1]
    for at in range(back_ref.shape[0]):
        lanes = slice(at * width, (at + 1) * width)
        back = back_ref[at].astype(jnp.float32).T
        for factor_ref, out_ref in zip(refs[:count], refs[count:]):
            factor = factor_ref[:, lanes].astype(jnp.float32)
            out_ref[:, lanes] = (back * factor).astype(jnp.bfloat16)


def ungate(back, factors):
    count, width, rows = back.shape
    columns = count * width
    if width % 128 != 0:
        part = back.transpose(2, 0, 1).reshape(rows, columns).astype(jnp.float32)
        return [(part * factor.astype(jnp.float32)).astype(jnp.bfloat16) for factor in factors]
    group = math.gcd(count, 4)
    wide = pl.BlockSpec((rows, group * width), lambda i: (0, i))
    return pl.pallas_call(
        ungate_kernel,
        grid=(count // group,),
        in_specs=[pl.BlockSpec((group, width, rows), lambda i: (i, 0, 0))]
        + [wide] * len(factors),
        out_specs=[wide] * len(factors),
        out_shape=[jax.ShapeDtypeStruct((rows, columns), jnp.bfloat16)] * len(factors),
        compiler_params=params(),
        cost_estimate=estimate(rows * columns, rows * columns * (2 + 4 * len(factors))),
    )(back, *factors)


def gather_all(block, count, index, inner):
    def swaps(held, masks):
        received = [held]
        for mask in masks:
            pairs = [(i, i ^ mask) for i in range(count)]
            received.append(lax.ppermute(held, "seq", pairs))
        return jnp.stack(received)

    across = swaps(block, range(inner, count, inner))
    held = swaps(across, range(1, inner))
    bits = count.bit_length() - 1
    inner_bits = inner.bit_length() - 1
    held = held.reshape((2,) * bits + block.shape)
    for axis in range(bits):
        bit = inner_bits - 1 - axis if axis < inner_bits else bits - 1 - (axis - inner_bits)
        held = jnp.where((index >> bit) % 2 == 1, jnp.flip(held, axis), held)
    held = held.reshape((inner, count // inner) + block.shape)
    return jnp.swapaxes(held, 0, 1).reshape((count,) + block.shape), across


def per_device(q_proj, k_proj, v_proj, grad_out, w_first, w_second, decay_rate, skip_gain):
    height, chan_tp = q_proj.shape
    parts = lax.axis_size("seq")
    length = height * parts
    width = chan_tp // parts
    band_total, hidden_count = w_first.shape
    seq_index = lax.axis_index("seq")

    def exchange(values):
        return lax.all_to_all(values, "seq", split_axis=0, concat_axis=0, tiled=True)

    gated_in = exchange(gate(k_proj, v_proj, parts))
    gated_grad = gate(grad_out, q_proj, parts)

    tables = jnp.asarray(transform_tables(length, height))
    twiddle = jnp.asarray(twiddle_table(length, height))
    positional = positional_table(length, band_total // 2)
    sine_input = jnp.dot(
        w_first.T, positional, precision=HIGH, preferred_element_type=jnp.float32
    )
    hidden = jnp.sin(sine_input)
    cosine = jnp.cos(sine_input)
    offset = seq_index * width
    w_mine = lax.dynamic_slice_in_dim(w_second, offset, width, 1)
    decay_mine = lax.dynamic_slice_in_dim(decay_rate, offset, width, 0)[:, None]
    skip_mine = lax.dynamic_slice_in_dim(skip_gain, offset, width, 0)[:, None]

    spectrum_shape = jax.ShapeDtypeStruct((parts, width, 2 * height), jnp.float32)
    work = pltpu.VMEM(spectrum_shape.shape, jnp.float32)
    split = pltpu.VMEM((2, 6 * height, 2 * height), jnp.bfloat16)
    anywhere = pl.BlockSpec(memory_space=pl.ANY)
    in_vmem = pl.BlockSpec(memory_space=pltpu.VMEM)
    product_flops = 2 * 3 * parts * 4 * height * height * width

    long_filter, filter_spectrum = pl.pallas_call(
        filter_kernel,
        in_specs=[in_vmem] * 5,
        out_specs=[in_vmem, in_vmem],
        out_shape=[jax.ShapeDtypeStruct((width, length), jnp.float32), spectrum_shape],
        scratch_shapes=[work, split],
        compiler_params=params(),
        cost_estimate=estimate(1000, 1000),
    )(w_mine.T, hidden, decay_mine, tables, twiddle)

    gated_grad, long_filter, filter_spectrum, w_mine, skip_mine, positional = (
        lax.optimization_barrier(
            (gated_grad, long_filter, filter_spectrum, w_mine, skip_mine, positional)
        )
    )
    gated_grad = exchange(gated_grad)
    sems = pltpu.SemaphoreType.DMA((2,))
    block_shape = jax.ShapeDtypeStruct(gated_in.shape, jnp.bfloat16)

    convolved, in_spectrum = pl.pallas_call(
        conv_kernel,
        in_specs=[in_vmem, anywhere, in_vmem, in_vmem, in_vmem],
        out_specs=[in_vmem, anywhere],
        out_shape=[block_shape, spectrum_shape],
        scratch_shapes=[work, work, work, split, sems],
        compiler_params=params(),
        cost_estimate=estimate(2 * product_flops, length * width * 20),
    )(gated_in, filter_spectrum, tables, twiddle, skip_mine)
    conv_back = exchange(convolved)

    grad_gated, small, first_pair = pl.pallas_call(
        grad_kernel,
        in_specs=[in_vmem, in_vmem, anywhere, anywhere, anywhere] + [in_vmem] * 8,
        out_specs=[in_vmem, in_vmem, in_vmem],
        out_shape=[
            block_shape,
            jax.ShapeDtypeStruct((hidden_count + 16, width), jnp.bfloat16),
            jax.ShapeDtypeStruct((2 * band_total, hidden_count), jnp.bfloat16),
        ],
        scratch_shapes=[
            work,
            work,
            work,
            pltpu.VMEM((width, length), jnp.float32),
            pltpu.VMEM((2, width, height), jnp.float32),
            split,
            pltpu.SemaphoreType.DMA((3,)),
        ],
        compiler_params=params(),
        cost_estimate=estimate(3 * product_flops, length * width * 20),
    )(
        gated_in,
        gated_grad,
        in_spectrum,
        filter_spectrum,
        long_filter,
        tables,
        twiddle,
        skip_mine,
        decay_mine,
        hidden,
        w_mine,
        cosine,
        positional,
    )
    packed = jnp.concatenate([small, first_pair.reshape(-1, width)], axis=0)
    gathered, across = gather_all(packed, parts, seq_index, math.gcd(parts, 4))
    grad_gated, _ = lax.optimization_barrier((grad_gated, across))
    grad_back = exchange(grad_gated)
    second = gathered[:, :hidden_count].astype(jnp.float32)
    grad_second = second.transpose(1, 0, 2).reshape(hidden_count, chan_tp)
    tail = gathered[:, hidden_count : hidden_count + 4].astype(jnp.float32)
    grad_decay = (tail[:, 0] + tail[:, 1]).reshape(chan_tp)
    grad_skip = (tail[:, 2] + tail[:, 3]).reshape(chan_tp)
    first_rows = gathered[:, hidden_count + 16 :].astype(jnp.float32).sum(axis=0)
    grad_first = first_rows.reshape(2, band_total, hidden_count).sum(axis=0)
    if lax.axis_size("tp") == 2:
        grad_first = grad_first + lax.ppermute(grad_first, "tp", [(0, 1), (1, 0)])
    else:
        grad_first = lax.psum(grad_first, "tp")
    (grad_q,) = ungate(conv_back, (grad_out,))
    grad_k, grad_v = ungate(grad_back, (v_proj, k_proj))
    return (grad_q, grad_k, grad_v, grad_first, grad_second, grad_decay, grad_skip)


def solution(mesh):
    return jax.shard_map(
        per_device,
        mesh=mesh,
        in_specs=(
            P("seq", "tp"),
            P("seq", "tp"),
            P("seq", "tp"),
            P("seq", "tp"),
            P(),
            P(None, "tp"),
            P("tp"),
            P("tp"),
        ),
        out_specs=(
            P("seq", "tp"),
            P("seq", "tp"),
            P("seq", "tp"),
            P(),
            P(None, "tp"),
            P("tp"),
            P("tp"),
        ),
        check_vma=False,
    )
```

profile of v0, /device:TPU:0, one launch (start us, length us, event | category | flops | bytes accessed | tf_op | source)
XLA Modules:
  0.0 138.6 jit_solution(1776599325327189536)
XLA Ops:
  0.7 3.9 %shard_map.153 = bf16[16,256,128]{2,1,0:T(8,128)(2,1)} custom-call(bf16[128,4096]{1,0:T(8,128)(2,1)} %refs_1_.1, bf16[128,4096]{1,0:T(8,128)(2,1)} %refs_0_.3), custom_call_target="tpu_custom_call" | custom-call | flops 524288 | bytes 3145728 | tf_op jit(solution)/shard_map/pallas_call | solution.py:405
  4.5 7.4 %all-to-all-start = ((bf16[16,256,128]{2,1,0:T(8,128)(2,1)}), bf16[16,256,128]{2,1,0:T(8,128)(2,1)S(1)}, u32[]{:S(2)}, u32[]{:S(2)}) async-start(bf16[16,256,128]{2,1,0:T(8,128)(2,1)} %shard_map.153), calls=%async_computation | async-start | bytes 2097152 | tf_op jit(solution)/shard_map/all_to_all | solution.py:476
  13.5 0.8 copy.26.decay_ref
  14.9 3.4 %cosine_bitcast_fusion = (f32[64,2048]{1,0:T(8,128)}, f32[64,2048]{1,0:T(8,128)}) fusion(f32[32,64]{1,0:T(8,128)S(1)} %copy-done.5, f32[16,2048]{1,0:T(8,128)S(1)} %get-tuple-element.46, f32[16,2048]{1,0:T(8,128)S(1)} %get-tuple-element.45), kind=kOutput, calls=%fused_computation.6 | convolution fusion | flops 50397184 | bytes 1318912 | tf_op jit(solution)/shard_map/dot_general | solution.py:484
  18.3 9.7 %shard_map.155 = (f32[256,2048]{1,0:T(8,128)}, f32[16,256,256]{2,1,0:T(8,128)}) custom-call(f32[256,64]{1,0:T(8,128)} %copy.25.w_t_ref, f32[64,2048]{1,0:T(8,128)} %get-tuple-element.40.hidden_ref, f32[256,1]{1,0:T(8,128)} %copy.26.decay_ref, f32[2,256,256]{2,1,0:T(8,128)} %constant.63.clone.table_ref, f32[16,256]{1,0:T(8,128)} %constant.64.clone.twiddle_ref), custom_call_target="tpu_custom_call" | custom-call | flops 1000 | bytes 1000 | tf_op jit(solution)/shard_map/pallas_call | solution.py:501
  28.8 3.8 %shard_map.154 = bf16[16,256,128]{2,1,0:T(8,128)(2,1)} custom-call(bf16[128,4096]{1,0:T(8,128)(2,1)} %refs_0_.2, bf16[128,4096]{1,0:T(8,128)(2,1)} %right_ref.3), custom_call_target="tpu_custom_call" | custom-call | flops 524288 | bytes 3145728 | tf_op jit(solution)/shard_map/pallas_call | solution.py:405
  33.9 0.9 all-to-all-done.x_ref
  34.9 6.9 %all-to-all-start.2 = ((bf16[16,256,128]{2,1,0:T(8,128)(2,1)}), bf16[16,256,128]{2,1,0:T(8,128)(2,1)S(1)}, u32[]{:S(2)}, u32[]{:S(2)}) async-start(bf16[16,256,128]{2,1,0:T(8,128)(2,1)} %shard_map.154), calls=%async_computation.2 | async-start | bytes 2097152 | tf_op jit(solution)/shard_map/all_to_all | solution.py:476
  41.7 0.8 copy.27.skip_ref
  42.5 12.9 %shard_map.156 = (bf16[16,256,128]{2,1,0:T(8,128)(2,1)}, f32[16,256,256]{2,1,0:T(8,128)}) custom-call(bf16[16,256,128]{2,1,0:T(8,128)(2,1)} %copy-done.3, f32[16,256,256]{2,1,0:T(8,128)} %get-tuple-element.25.h_any, f32[2,256,256]{2,1,0:T(8,128)} %constant.63.clone.table_ref, f32[16,256]{1,0:T(8,128)} %constant.64.clone.twiddle_ref, f32[256,1]{1,0:T(8,128)} %copy.27.skip_ref), custom_call_target="tpu_custom_call" | custom-call | flops 3221225472 | bytes 10485760 | tf_op jit(solution)/shard_map/pallas_call | solution.py:520
  55.4 9.2 %all-to-all-done.2.g_ref = bf16[16,256,128]{2,1,0:T(8,128)(2,1)S(1)} async-done(((bf16[16,256,128]{2,1,0:T(8,128)(2,1)}), bf16[16,256,128]{2,1,0:T(8,128)(2,1)S(1)}, u32[]{:S(2)}, u32[]{:S(2)}) %all-to-all-start.2) | async-done | bytes 1048608 | tf_op jit(solution)/shard_map/all_to_all | solution.py:476
  64.7 1.0 copy-done.4
  65.7 6.9 %all-to-all-start.1 = ((bf16[16,256,128]{2,1,0:T(8,128)(2,1)}), bf16[16,256,128]{2,1,0:T(8,128)(2,1)S(1)}, u32[]{:S(2)}, u32[]{:S(2)}) async-start(bf16[16,256,128]{2,1,0:T(8,128)(2,1)} %get-tuple-element.27), calls=%async_computation.1 | async-start | bytes 2097152 | tf_op jit(solution)/shard_map/all_to_all | solution.py:476
  72.5 19.0 %shard_map.158 = (bf16[16,256,128]{2,1,0:T(8,128)(2,1)}, bf16[80,256]{1,0:T(8,128)(2,1)}, bf16[64,64]{1,0:T(8,128)(2,1)}) custom-call(bf16[16,256,128]{2,1,0:T(8,128)(2,1)} %copy-done.3, bf16[16,256,128]{2,1,0:T(8,128)(2,1)} %copy-done.4, f32[16,256,256]{2,1,0:T(8,128)} %get-tuple-element.29.x_any, f32[16,256,256]{2,1,0:T(8,128)} %get-tuple-element.25.h_any, ...), custom_call_target="tpu_custom_call" | custom-call | flops 4831838208 | bytes 10485760 | tf_op jit(solution)/shard_map/pallas_call | solution.py:531
  91.5 0.8 reshape.51
  92.4 0.8 constant_dynamic-update-slice_fusion.1
  93.1 3.7 %collective-permute-start.2 = (bf16[96,256]{1,0:T(8,128)(2,1)S(1)}, bf16[96,256]{1,0:T(8,128)(2,1)S(1)}, u32[]{:S(2)}, u32[]{:S(2)}) collective-permute-start(bf16[96,256]{1,0:T(8,128)(2,1)S(1)} %constant_dynamic-update-slice_fusion), channel_id=1, source_target_pairs={{0,24},{2,26},{4,28},{6,30},{8,16},{10,18},{12,20},{14,22},{16,8},... | collective-permute-start | bytes 147464 | tf_op jit(solution)/shard_map/ppermute | solution.py:452
  97.5 1.6 %collective-permute-done.2 = bf16[96,256]{1,0:T(8,128)(2,1)S(1)} collective-permute-done((bf16[96,256]{1,0:T(8,128)(2,1)S(1)}, bf16[96,256]{1,0:T(8,128)(2,1)S(1)}, u32[]{:S(2)}, u32[]{:S(2)}) %collective-permute-start.2) | collective-permute-done | bytes 49184 | tf_op jit(solution)/shard_map/ppermute | solution.py:452
  99.1 4.2 %collective-permute-done.1 = bf16[96,256]{1,0:T(8,128)(2,1)S(1)} collective-permute-done((bf16[96,256]{1,0:T(8,128)(2,1)S(1)}, bf16[96,256]{1,0:T(8,128)(2,1)S(1)}, u32[]{:S(2)}, u32[]{:S(2)}) %collective-permute-start.1) | collective-permute-done | bytes 49184 | tf_op jit(solution)/shard_map/ppermute | solution.py:452
  104.7 0.8 collective-permute-start.4
  105.9 3.7 %all-to-all-start.3 = ((bf16[16,256,128]{2,1,0:T(8,128)(2,1)}), bf16[16,256,128]{2,1,0:T(8,128)(2,1)S(1)}, u32[]{:S(2)}, u32[]{:S(2)}) async-start(bf16[16,256,128]{2,1,0:T(8,128)(2,1)} %get-tuple-element.36), calls=%async_computation.3 | async-start | bytes 2097152 | tf_op jit(solution)/shard_map/all_to_all | solution.py:476
  109.6 1.8 %collective-permute-done.5 = bf16[4,96,256]{2,1,0:T(8,128)(2,1)S(1)} collective-permute-done((bf16[4,96,256]{2,1,0:T(8,128)(2,1)}, bf16[4,96,256]{2,1,0:T(8,128)(2,1)S(1)}, u32[]{:S(2)}, u32[]{:S(2)}) %collective-permute-start.5) | collective-permute-done | bytes 196640 | tf_op jit(solution)/shard_map/ppermute | solution.py:452
  111.4 6.8 %collective-permute-done.4 = bf16[4,96,256]{2,1,0:T(8,128)(2,1)} collective-permute-done((bf16[4,96,256]{2,1,0:T(8,128)(2,1)}, bf16[4,96,256]{2,1,0:T(8,128)(2,1)}, u32[]{:S(2)}, u32[]{:S(2)}) %collective-permute-start.4) | collective-permute-done | bytes 196640 | tf_op jit(solution)/shard_map/ppermute | solution.py:452
  118.1 1.1 pad_maximum_fusion
  120.6 1.1 reshape.54
  121.6 0.9 convert_reduce_fusion
  122.7 1.6 %collective-permute-start.6 = (f32[32,64]{1,0:T(8,128)S(1)}, f32[32,64]{1,0:T(8,128)S(1)}, u32[]{:S(2)}, u32[]{:S(2)}) collective-permute-start(f32[32,64]{1,0:T(8,128)S(1)} %reduce_sum.19), channel_id=1, source_target_pairs={{0,1},{1,0},{2,3},{3,2},{4,5},{5,4},{6,7},{7,6},{8,9},{9,8},{10,11... | collective-permute-start | bytes 24584 | tf_op jit(solution)/shard_map/ppermute | solution.py:578
  125.0 1.2 slice_convert_fusion
  126.2 1.6 %copy.31 = f32[8,8,16,256]{3,1,2,0:T(8,128)} copy(f32[8,8,16,256]{3,2,1,0:T(8,128)S(1)} %bitcast.35) | data formatting | bytes 2097152
  129.6 3.8 %shard_map.157 = bf16[128,4096]{1,0:T(8,128)(2,1)} custom-call(bf16[16,256,128]{2,1,0:T(8,128)(2,1)} %copy-done.1, bf16[128,4096]{1,0:T(8,128)(2,1)} %refs_0_.2), custom_call_target="tpu_custom_call" | custom-call | flops 524288 | bytes 3145728 | tf_op jit(solution)/shard_map/pallas_call | solution.py:435
  133.4 1.0 copy-done.2
  134.4 4.2 %shard_map.159 = (bf16[128,4096]{1,0:T(8,128)(2,1)}, bf16[128,4096]{1,0:T(8,128)(2,1)}) custom-call(bf16[16,256,128]{2,1,0:T(8,128)(2,1)} %copy-done.2, bf16[128,4096]{1,0:T(8,128)(2,1)} %refs_0_.3, bf16[128,4096]{1,0:T(8,128)(2,1)} %refs_1_.1), custom_call_target="tpu_custom_call" | custom-call | flops 524288 | bytes 5242880 | tf_op jit(solution)/shard_map/pallas_call | solution.py:435
  (41 shorter events, 10.7 us)
Async XLA Ops:
  0.6 11.3 %copy-start = (f32[64,4096]{1,0:T(8,128)S(1)}, f32[64,4096]{1,0:T(8,128)}, u32[]{:S(2)}) copy-start(f32[64,4096]{1,0:T(8,128)} %param.15) | copy-start | bytes 3145732
  0.6 14.2 %copy-start.5 = (f32[32,64]{1,0:T(8,128)S(1)}, f32[32,64]{1,0:T(8,128)}, u32[]{:S(2)}) copy-start(f32[32,64]{1,0:T(8,128)} %param.14) | copy-start | bytes 24580
  4.5 30.3 %all-to-all-start = ((bf16[16,256,128]{2,1,0:T(8,128)(2,1)}), bf16[16,256,128]{2,1,0:T(8,128)(2,1)S(1)}, u32[]{:S(2)}, u32[]{:S(2)}) async-start(bf16[16,256,128]{2,1,0:T(8,128)(2,1)} %shard_map.153), calls=%async_computation | async-start | bytes 2097152 | tf_op jit(solution)/shard_map/all_to_all | solution.py:476
  34.9 7.7 %copy-start.3 = (bf16[16,256,128]{2,1,0:T(8,128)(2,1)}, bf16[16,256,128]{2,1,0:T(8,128)(2,1)S(1)}, u32[]{:S(2)}) copy-start(bf16[16,256,128]{2,1,0:T(8,128)(2,1)S(1)} %all-to-all-done.x_ref) | copy-start | bytes 3145732
  34.9 29.8 %all-to-all-start.2 = ((bf16[16,256,128]{2,1,0:T(8,128)(2,1)}), bf16[16,256,128]{2,1,0:T(8,128)(2,1)S(1)}, u32[]{:S(2)}, u32[]{:S(2)}) async-start(bf16[16,256,128]{2,1,0:T(8,128)(2,1)} %shard_map.154), calls=%async_computation.2 | async-start | bytes 2097152 | tf_op jit(solution)/shard_map/all_to_all | solution.py:476
  64.7 1.0 copy-start.4
  65.7 40.2 %all-to-all-start.1 = ((bf16[16,256,128]{2,1,0:T(8,128)(2,1)}), bf16[16,256,128]{2,1,0:T(8,128)(2,1)S(1)}, u32[]{:S(2)}, u32[]{:S(2)}) async-start(bf16[16,256,128]{2,1,0:T(8,128)(2,1)} %get-tuple-element.27), calls=%async_computation.1 | async-start | bytes 2097152 | tf_op jit(solution)/shard_map/all_to_all | solution.py:476
  93.1 6.0 %collective-permute-start.2 = (bf16[96,256]{1,0:T(8,128)(2,1)S(1)}, bf16[96,256]{1,0:T(8,128)(2,1)S(1)}, u32[]{:S(2)}, u32[]{:S(2)}) collective-permute-start(bf16[96,256]{1,0:T(8,128)(2,1)S(1)} %constant_dynamic-update-slice_fusion), channel_id=1, source_target_pairs={{0,24},{2,26},{4,28},{6,30},{8,16},{10,18},{12,20},{14,22},{16,8},... | collective-permute-start | bytes 147464 | tf_op jit(solution)/shard_map/ppermute | solution.py:452
  96.9 6.4 %collective-permute-start.1 = (bf16[96,256]{1,0:T(8,128)(2,1)S(1)}, bf16[96,256]{1,0:T(8,128)(2,1)S(1)}, u32[]{:S(2)}, u32[]{:S(2)}) collective-permute-start(bf16[96,256]{1,0:T(8,128)(2,1)S(1)} %constant_dynamic-update-slice_fusion), channel_id=1, source_target_pairs={{0,16},{2,18},{4,20},{6,22},{8,24},{10,26},{12,28},{14,30},{16,0},... | collective-permute-start | bytes 147464 | tf_op jit(solution)/shard_map/ppermute | solution.py:452
  96.9 6.4 %collective-permute-start = (bf16[96,256]{1,0:T(8,128)(2,1)S(1)}, bf16[96,256]{1,0:T(8,128)(2,1)S(1)}, u32[]{:S(2)}, u32[]{:S(2)}) collective-permute-start(bf16[96,256]{1,0:T(8,128)(2,1)S(1)} %constant_dynamic-update-slice_fusion), channel_id=1, source_target_pairs={{0,8},{2,10},{4,12},{6,14},{8,0},{10,2},{12,4},{14,6},{16,24},{18,... | collective-permute-start | bytes 147464 | tf_op jit(solution)/shard_map/ppermute | solution.py:452
  104.0 7.4 %collective-permute-start.5 = (bf16[4,96,256]{2,1,0:T(8,128)(2,1)}, bf16[4,96,256]{2,1,0:T(8,128)(2,1)S(1)}, u32[]{:S(2)}, u32[]{:S(2)}) collective-permute-start(bf16[4,96,256]{2,1,0:T(8,128)(2,1)} %get-tuple-element.42), channel_id=1, source_target_pairs={{0,6},{2,4},{4,2},{6,0},{8,14},{10,12},{12,10},{14,8},{16,22},{18,... | collective-permute-start | bytes 589832 | tf_op jit(solution)/shard_map/ppermute | solution.py:452
  104.7 13.4 %collective-permute-start.4 = (bf16[4,96,256]{2,1,0:T(8,128)(2,1)}, bf16[4,96,256]{2,1,0:T(8,128)(2,1)}, u32[]{:S(2)}, u32[]{:S(2)}) collective-permute-start(bf16[4,96,256]{2,1,0:T(8,128)(2,1)} %get-tuple-element.42), channel_id=1, source_target_pairs={{0,4},{2,6},{4,0},{6,2},{8,12},{10,14},{12,8},{14,10},{16,20},{18,... | collective-permute-start | bytes 589832 | tf_op jit(solution)/shard_map/ppermute | solution.py:452
  105.5 12.6 %collective-permute-start.3 = (bf16[4,96,256]{2,1,0:T(8,128)(2,1)}, bf16[4,96,256]{2,1,0:T(8,128)(2,1)}, u32[]{:S(2)}, u32[]{:S(2)}) collective-permute-start(bf16[4,96,256]{2,1,0:T(8,128)(2,1)} %get-tuple-element.42), channel_id=1, source_target_pairs={{0,2},{2,0},{4,6},{6,4},{8,10},{10,8},{12,14},{14,12},{16,18},{18,... | collective-permute-start | bytes 589832 | tf_op jit(solution)/shard_map/ppermute | solution.py:452
  105.9 13.9 %copy-start.1 = (bf16[16,256,128]{2,1,0:T(8,128)(2,1)}, bf16[16,256,128]{2,1,0:T(8,128)(2,1)S(1)}, u32[]{:S(2)}) copy-start(bf16[16,256,128]{2,1,0:T(8,128)(2,1)S(1)} %all-to-all-done.1.back_ref) | copy-start | bytes 3145732
  105.9 27.5 %all-to-all-start.3 = ((bf16[16,256,128]{2,1,0:T(8,128)(2,1)}), bf16[16,256,128]{2,1,0:T(8,128)(2,1)S(1)}, u32[]{:S(2)}, u32[]{:S(2)}) async-start(bf16[16,256,128]{2,1,0:T(8,128)(2,1)} %get-tuple-element.36), calls=%async_computation.3 | async-start | bytes 2097152 | tf_op jit(solution)/shard_map/all_to_all | solution.py:476
  122.7 6.3 %collective-permute-start.6 = (f32[32,64]{1,0:T(8,128)S(1)}, f32[32,64]{1,0:T(8,128)S(1)}, u32[]{:S(2)}, u32[]{:S(2)}) collective-permute-start(f32[32,64]{1,0:T(8,128)S(1)} %reduce_sum.19), channel_id=1, source_target_pairs={{0,1},{1,0},{2,3},{3,2},{4,5},{5,4},{6,7},{7,6},{8,9},{9,8},{10,11... | collective-permute-start | bytes 24584 | tf_op jit(solution)/shard_map/ppermute | solution.py:578
  133.4 1.0 copy-start.2
where the time goes:
time: 140 us; the launch traced here: 139 us
  Pallas kernels  57.2 us (41%)
  starting transfers between devices  32.7 us (23%)
  waiting for transfers between devices  24.5 us (18%)
  local copies, waits for them, and re-layouts  12.6 us (9%)
  other arithmetic  7.3 us (5%)
  matrix products  3.44 us (2%)
    all_to_all x4, starting transfers between devices, exchange(): lax.all_to_all(values, 'seq', split_axis=0, concat_axis=0, tiled=True)  24.9 us
    pallas_call x1, Pallas kernels, per_device(): pl.pallas_call(grad_kernel, in_specs=[in_vmem, in_vmem, anywhere, anywher...  19 us
    ppermute x6, waiting for transfers between devices, swaps(): received.append(lax.ppermute(held, 'seq', pairs))  14.3 us
    pallas_call x1, Pallas kernels, per_device(): pl.pallas_call(conv_kernel, in_specs=[in_vmem, anywhere, in_vmem, in_vmem...  12.9 us
    all_to_all x4, waiting for transfers between devices, exchange(): lax.all_to_all(values, 'seq', split_axis=0, concat_axis=0, tiled=True)  10.2 us
    pallas_call x1, Pallas kernels, per_device(): pl.pallas_call(filter_kernel, in_specs=[in_vmem] * 5, out_specs=[in_vmem,...  9.71 us
    pallas_call x2, Pallas kernels, ungate(): pl.pallas_call(ungate_kernel, grid=(count // group,), in_specs=[pl.BlockS...  7.98 us
    pallas_call x2, Pallas kernels, gate(): pl.pallas_call(gate_kernel, grid=(count // group,), in_specs=[pl.BlockSpe...  7.66 us
  transfers between devices with their start and end apart: 11, of which 6 were waited for; matrix products, arithmetic and copies ran while one was open for 15% of the time, Pallas kernels for 35%

commit v1 on v0

--- a/solution.py
+++ b/solution.py
@@ -378,21 +378,65 @@
     small_ref[hidden_count:, :] = tail.astype(jnp.bfloat16)
 
 
-def params():
-    return pltpu.CompilerParams(vmem_limit_bytes=56 * MIB)
+def params(limit=56):
+    return pltpu.CompilerParams(vmem_limit_bytes=limit * MIB)
 
 
 def estimate(flops, nbytes):
     return pl.CostEstimate(flops=flops, bytes_accessed=nbytes, transcendentals=0)
 
 
-def gate_kernel(left_ref, right_ref, out_ref):
-    width = out_ref.shape[1]
-    for at in range(out_ref.shape[0]):
-        lanes = slice(at * width, (at + 1) * width)
+def chunk_copies(pairs, sems, first):
+    return [
+        [
+            pltpu.make_async_copy(source, target, sems.at[first + at * len(chunk) + which])
+            for which, (source, target) in enumerate(chunk)
+        ]
+        for at, chunk in enumerate(pairs)
+    ]
+
+
+def run_streams(blocks, group, width, shared, wide_in, wide_out, shared_out, sems, work):
+    def part(refs, at):
+        return [ref.at[pl.ds(at * group, group)] for ref in refs]
+
+    def lanes(refs, at):
+        return [ref.at[:, pl.ds(at * group * width, group * width)] for ref in refs]
+
+    chunks = range(blocks // group)
+    incoming, outgoing = [], []
+    for at in chunks:
+        pairs = [tuple(part(pair, at)) for pair in shared]
+        incoming.append(pairs + [tuple(lanes(pair, at)) for pair in wide_in])
+        pairs = [tuple(part(pair, at)) for pair in shared_out]
+        outgoing.append(pairs + [tuple(lanes(pair, at)) for pair in wide_out])
+    arrivals = chunk_copies(incoming, sems, 0)
+    departures = chunk_copies(outgoing, sems, len(arrivals) * len(arrivals[0]))
+    for chunk in arrivals:
+        for copy in chunk:
+            copy.start()
+    for at in chunks:
+        for copy in arrivals[at]:
+            copy.wait()
+        for block in range(at * group, (at + 1) * group):
+            work(block, slice(block * width, (block + 1) * width))
+        for copy in departures[at]:
+            copy.start()
+    for chunk in departures:
+        for copy in chunk:
+            copy.wait()
+
+
+def gate_kernel(group, left_any, right_any, out_any, left_ref, right_ref, out_ref, sems):
+    count, width, _ = out_ref.shape
+
+    def work(block, lanes):
         left = left_ref[:, lanes].astype(jnp.float32)
         right = right_ref[:, lanes].astype(jnp.float32)
-        out_ref[at] = (left * right).T.astype(jnp.bfloat16)
+        out_ref[block] = (left * right).T.astype(jnp.bfloat16)
+
+    wide = [(left_any, left_ref), (right_any, right_ref)]
+    run_streams(count, group, width, [], wide, [], [(out_ref, out_any)], sems, work)
 
 
 def gate(left, right, count):
@@ -401,27 +445,42 @@
     if width % 128 != 0:
         product = (left.astype(jnp.float32) * right.astype(jnp.float32)).astype(jnp.bfloat16)
         return product.reshape(rows, count, width).transpose(1, 2, 0)
-    group = math.gcd(count, 4)
+    group = math.gcd(count, 2)
+    out = jax.ShapeDtypeStruct((count, width, rows), jnp.bfloat16)
+    wide = pltpu.VMEM((rows, columns), jnp.bfloat16)
     return pl.pallas_call(
-        gate_kernel,
-        grid=(count // group,),
-        in_specs=[pl.BlockSpec((rows, group * width), lambda i: (0, i))] * 2,
-        out_specs=pl.BlockSpec((group, width, rows), lambda i: (i, 0, 0)),
-        out_shape=jax.ShapeDtypeStruct((count, width, rows), jnp.bfloat16),
-        compiler_params=params(),
+        functools.partial(gate_kernel, group),
+        in_specs=[pl.BlockSpec(memory_space=pl.ANY)] * 2,
+        out_specs=pl.BlockSpec(memory_space=pl.ANY),
+        out_shape=out,
+        scratch_shapes=[
+            wide,
+            wide,
+            pltpu.VMEM(out.shape, jnp.bfloat16),
+            pltpu.SemaphoreType.DMA((3 * count // group,)),
+        ],
+        compiler_params=params(16),
         cost_estimate=estimate(rows * columns, rows * columns * 6),
     )(left, right)
 
 
-def ungate_kernel(back_ref, *refs):
-    count = len(refs) // 2
-    width = back_ref.shape[1]
-    for at in range(back_ref.shape[0]):
-        lanes = slice(at * width, (at + 1) * width)
-        back = back_ref[at].astype(jnp.float32).T
-        for factor_ref, out_ref in zip(refs[:count], refs[count:]):
+def ungate_kernel(group, factors, *refs):
+    back_any, factor_anys = refs[0], refs[1 : factors + 1]
+    out_anys = refs[factors + 1 : 2 * factors + 1]
+    back_ref, *rest = refs[2 * factors + 1 :]
+    factor_refs, out_refs, sems = rest[:factors], rest[factors:-1], rest[-1]
+    count, width, _ = back_ref.shape
+
+    def work(block, lanes):
+        back = back_ref[block].astype(jnp.float32).T
+        for factor_ref, out_ref in zip(factor_refs, out_refs):
             factor = factor_ref[:, lanes].astype(jnp.float32)
             out_ref[:, lanes] = (back * factor).astype(jnp.bfloat16)
+
+    shared = [(back_any, back_ref)]
+    wide_in = list(zip(factor_anys, factor_refs))
+    wide_out = list(zip(out_refs, out_anys))
+    run_streams(count, group, width, shared, wide_in, wide_out, [], sems, work)
 
 
 def ungate(back, factors):
@@ -430,16 +489,19 @@
     if width % 128 != 0:
         part = back.transpose(2, 0, 1).reshape(rows, columns).astype(jnp.float32)
         return [(part * factor.astype(jnp.float32)).astype(jnp.bfloat16) for factor in factors]
-    group = math.gcd(count, 4)
-    wide = pl.BlockSpec((rows, group * width), lambda i: (0, i))
+    group = math.gcd(count, 2)
+    anywhere = pl.BlockSpec(memory_space=pl.ANY)
+    wide = pltpu.VMEM((rows, columns), jnp.bfloat16)
+    copies = (1 + 2 * len(factors)) * count // group
     return pl.pallas_call(
-        ungate_kernel,
-        grid=(count // group,),
-        in_specs=[pl.BlockSpec((group, width, rows), lambda i: (i, 0, 0))]
-        + [wide] * len(factors),
-        out_specs=[wide] * len(factors),
+        functools.partial(ungate_kernel, group, len(factors)),
+        in_specs=[anywhere] * (1 + len(factors)),
+        out_specs=[anywhere] * len(factors),
         out_shape=[jax.ShapeDtypeStruct((rows, columns), jnp.bfloat16)] * len(factors),
-        compiler_params=params(),
+        scratch_shapes=[pltpu.VMEM(back.shape, jnp.bfloat16)]
+        + [wide] * (2 * len(factors))
+        + [pltpu.SemaphoreType.DMA((copies,))],
+        compiler_params=params(16),
         cost_estimate=estimate(rows * columns, rows * columns * (2 + 4 * len(factors))),
     )(back, *factors)
 

time: 140 us -> 141 us (level)
  Pallas kernels: 57.2 us -> 52 us
  local copies, waits for them, and re-layouts: 12.6 us -> 17.7 us
    pallas_call x4, Pallas kernels: 15.6 us -> 10.4 us  [the longest x2 6.09 us: ungate(): pl.pallas_call(functools.partial(ungate_kernel, group, len(factors)), in_...]
    unnamed x16 -> x26, local copies, waits for them, and re-layouts: 5.57 us -> 8.4 us
    all_to_all x4, waiting for transfers between devices: 10.2 us -> 11.8 us  [exchange(): lax.all_to_all(values, 'seq', split_axis=0, concat_axis=0, tiled=True)]
  transfers between devices with their start and end apart: 11 -> 11, of which waited for: 6 -> 6; matrix products, arithmetic and copies ran while one was open for 15% -> 17% of each run, Pallas kernels for 35% -> 34%
where the time goes in v1:
time: 141 us; the launch traced here: 140 us
  Pallas kernels  52 us (37%)
  starting transfers between devices  33.3 us (24%)
  waiting for transfers between devices  25.2 us (18%)
  local copies, waits for them, and re-layouts  17.7 us (13%)
  other arithmetic  7.3 us (5%)
  matrix products  3.48 us (2%)
    all_to_all x4, starting transfers between devices, exchange(): lax.all_to_all(values, 'seq', split_axis=0, concat_axis=0, tiled=True)  25.5 us
    pallas_call x1, Pallas kernels, per_device(): pl.pallas_call(grad_kernel, in_specs=[in_vmem, in_vmem, anywhere, anywher...  19 us
    ppermute x6, waiting for transfers between devices, swaps(): received.append(lax.ppermute(held, 'seq', pairs))  13.4 us
    pallas_call x1, Pallas kernels, per_device(): pl.pallas_call(conv_kernel, in_specs=[in_vmem, anywhere, in_vmem, in_vmem...  12.9 us
    all_to_all x4, waiting for transfers between devices, exchange(): lax.all_to_all(values, 'seq', split_axis=0, concat_axis=0, tiled=True)  11.8 us
    pallas_call x1, Pallas kernels, per_device(): pl.pallas_call(filter_kernel, in_specs=[in_vmem] * 5, out_specs=[in_vmem,...  9.71 us
    unnamed x26, local copies, waits for them, and re-layouts  8.4 us
    ppermute x6, starting transfers between devices, swaps(): received.append(lax.ppermute(held, 'seq', pairs))  6.25 us
  transfers between devices with their start and end apart: 11, of which 6 were waited for; matrix products, arithmetic and copies ran while one was open for 17% of the time, Pallas kernels for 34%

profile of v1, /device:TPU:0, one launch (start us, length us, event | category | flops | bytes accessed | tf_op | source)
XLA Modules:
  0.0 140.0 jit_solution(822124725505809396)
XLA Ops:
  0.7 1.4 copy-done.2
  2.0 1.2 copy-done.4
  3.3 2.1 %shard_map.153 = bf16[16,256,128]{2,1,0:T(8,128)(2,1)} custom-call(bf16[128,4096]{1,0:T(8,128)(2,1)S(1)} %copy-done.2, bf16[128,4096]{1,0:T(8,128)(2,1)S(1)} %copy-done.4), custom_call_target="tpu_custom_call" | custom-call | flops 524288 | bytes 3145728 | tf_op jit(solution)/shard_map/pallas_call | solution.py:451
  5.4 7.4 %all-to-all-start = ((bf16[16,256,128]{2,1,0:T(8,128)(2,1)}), bf16[16,256,128]{2,1,0:T(8,128)(2,1)}, u32[]{:S(2)}, u32[]{:S(2)}) async-start(bf16[16,256,128]{2,1,0:T(8,128)(2,1)} %shard_map.153), calls=%async_computation | async-start | bytes 2097152 | tf_op jit(solution)/shard_map/all_to_all | solution.py:538
  14.4 0.8 copy.26.decay_ref
  15.8 3.5 %cosine_bitcast_fusion = (f32[64,2048]{1,0:T(8,128)}, f32[64,2048]{1,0:T(8,128)}) fusion(f32[32,64]{1,0:T(8,128)S(1)} %copy-done.10, f32[16,2048]{1,0:T(8,128)S(1)} %get-tuple-element.46, f32[16,2048]{1,0:T(8,128)S(1)} %get-tuple-element.45), kind=kOutput, calls=%fused_computation.6 | convolution fusion | flops 50397184 | bytes 1318912 | tf_op jit(solution)/shard_map/dot_general | solution.py:546
  19.3 9.7 %shard_map.155 = (f32[256,2048]{1,0:T(8,128)}, f32[16,256,256]{2,1,0:T(8,128)}) custom-call(f32[256,64]{1,0:T(8,128)} %copy.25.w_t_ref, f32[64,2048]{1,0:T(8,128)} %get-tuple-element.40.hidden_ref, f32[256,1]{1,0:T(8,128)} %copy.26.decay_ref, f32[2,256,256]{2,1,0:T(8,128)} %constant.63.clone.table_ref, f32[16,256]{1,0:T(8,128)} %constant.64.clone.twiddle_ref), custom_call_target="tpu_custom_call" | custom-call | flops 1000 | bytes 1000 | tf_op jit(solution)/shard_map/pallas_call | solution.py:563
  29.8 2.1 %shard_map.154 = bf16[16,256,128]{2,1,0:T(8,128)(2,1)} custom-call(bf16[128,4096]{1,0:T(8,128)(2,1)S(1)} %copy-done.1, bf16[128,4096]{1,0:T(8,128)(2,1)S(1)} %copy-done.8), custom_call_target="tpu_custom_call" | custom-call | flops 524288 | bytes 3145728 | tf_op jit(solution)/shard_map/pallas_call | solution.py:451
  33.3 2.5 %all-to-all-done.x_ref = bf16[16,256,128]{2,1,0:T(8,128)(2,1)} async-done(((bf16[16,256,128]{2,1,0:T(8,128)(2,1)}), bf16[16,256,128]{2,1,0:T(8,128)(2,1)}, u32[]{:S(2)}, u32[]{:S(2)}) %all-to-all-start) | async-done | bytes 1048608 | tf_op jit(solution)/shard_map/all_to_all | solution.py:538
  35.9 6.9 %all-to-all-start.2 = ((bf16[16,256,128]{2,1,0:T(8,128)(2,1)}), bf16[16,256,128]{2,1,0:T(8,128)(2,1)S(1)}, u32[]{:S(2)}, u32[]{:S(2)}) async-start(bf16[16,256,128]{2,1,0:T(8,128)(2,1)} %shard_map.154), calls=%async_computation.2 | async-start | bytes 2097152 | tf_op jit(solution)/shard_map/all_to_all | solution.py:538
  43.5 12.9 %shard_map.156 = (bf16[16,256,128]{2,1,0:T(8,128)(2,1)}, f32[16,256,256]{2,1,0:T(8,128)}) custom-call(bf16[16,256,128]{2,1,0:T(8,128)(2,1)} %all-to-all-done.x_ref, f32[16,256,256]{2,1,0:T(8,128)} %get-tuple-element.25.h_any, f32[2,256,256]{2,1,0:T(8,128)} %constant.63.clone.table_ref, f32[16,256]{1,0:T(8,128)} %constant.64.clone.twiddle_ref, ...), custom_call_target="tpu_custom_call" | custom-call | flops 3221225472 | bytes 10485760 | tf_op jit(solution)/shard_map/pallas_call | solution.py:582
  56.4 9.2 %all-to-all-done.2.g_ref = bf16[16,256,128]{2,1,0:T(8,128)(2,1)S(1)} async-done(((bf16[16,256,128]{2,1,0:T(8,128)(2,1)}), bf16[16,256,128]{2,1,0:T(8,128)(2,1)S(1)}, u32[]{:S(2)}, u32[]{:S(2)}) %all-to-all-start.2) | async-done | bytes 1048608 | tf_op jit(solution)/shard_map/all_to_all | solution.py:538
  65.7 1.0 copy-done.9
  66.6 6.9 %all-to-all-start.1 = ((bf16[16,256,128]{2,1,0:T(8,128)(2,1)}), bf16[16,256,128]{2,1,0:T(8,128)(2,1)S(1)}, u32[]{:S(2)}, u32[]{:S(2)}) async-start(bf16[16,256,128]{2,1,0:T(8,128)(2,1)} %get-tuple-element.27), calls=%async_computation.1 | async-start | bytes 2097152 | tf_op jit(solution)/shard_map/all_to_all | solution.py:538
  73.5 19.0 %shard_map.158 = (bf16[16,256,128]{2,1,0:T(8,128)(2,1)}, bf16[80,256]{1,0:T(8,128)(2,1)}, bf16[64,64]{1,0:T(8,128)(2,1)}) custom-call(bf16[16,256,128]{2,1,0:T(8,128)(2,1)} %all-to-all-done.x_ref, bf16[16,256,128]{2,1,0:T(8,128)(2,1)} %copy-done.9, f32[16,256,256]{2,1,0:T(8,128)} %get-tuple-element.29.x_any, f32[16,256,256]{2,1,0:T(8,128)} %get-tuple-element.25.h_any, ...), custom_call_target="tpu_custom_call" | custom-call | flops 4831838208 | bytes 10485760 | tf_op jit(solution)/shard_map/pallas_call | solution.py:593
  92.5 0.8 reshape.51
  94.1 3.7 %collective-permute-start.2 = (bf16[96,256]{1,0:T(8,128)(2,1)S(1)}, bf16[96,256]{1,0:T(8,128)(2,1)S(1)}, u32[]{:S(2)}, u32[]{:S(2)}) collective-permute-start(bf16[96,256]{1,0:T(8,128)(2,1)S(1)} %constant_dynamic-update-slice_fusion), channel_id=1, source_target_pairs={{0,24},{2,26},{4,28},{6,30},{8,16},{10,18},{12,20},{14,22},{16,8},... | collective-permute-start | bytes 147464 | tf_op jit(solution)/shard_map/ppermute | solution.py:514
  98.5 1.6 %collective-permute-done.2 = bf16[96,256]{1,0:T(8,128)(2,1)S(1)} collective-permute-done((bf16[96,256]{1,0:T(8,128)(2,1)S(1)}, bf16[96,256]{1,0:T(8,128)(2,1)S(1)}, u32[]{:S(2)}, u32[]{:S(2)}) %collective-permute-start.2) | collective-permute-done | bytes 49184 | tf_op jit(solution)/shard_map/ppermute | solution.py:514
  100.1 4.2 %collective-permute-done.1 = bf16[96,256]{1,0:T(8,128)(2,1)S(1)} collective-permute-done((bf16[96,256]{1,0:T(8,128)(2,1)S(1)}, bf16[96,256]{1,0:T(8,128)(2,1)S(1)}, u32[]{:S(2)}, u32[]{:S(2)}) %collective-permute-start.1) | collective-permute-done | bytes 49184 | tf_op jit(solution)/shard_map/ppermute | solution.py:514
  106.9 4.3 %all-to-all-start.3 = ((bf16[16,256,128]{2,1,0:T(8,128)(2,1)}), bf16[16,256,128]{2,1,0:T(8,128)(2,1)}, u32[]{:S(2)}, u32[]{:S(2)}) async-start(bf16[16,256,128]{2,1,0:T(8,128)(2,1)} %get-tuple-element.36), calls=%async_computation.3 | async-start | bytes 2097152 | tf_op jit(solution)/shard_map/all_to_all | solution.py:538
  111.2 1.2 collective-permute-done.5
  112.4 6.5 %collective-permute-done.4 = bf16[4,96,256]{2,1,0:T(8,128)(2,1)} collective-permute-done((bf16[4,96,256]{2,1,0:T(8,128)(2,1)}, bf16[4,96,256]{2,1,0:T(8,128)(2,1)}, u32[]{:S(2)}, u32[]{:S(2)}) %collective-permute-start.4) | collective-permute-done | bytes 196640 | tf_op jit(solution)/shard_map/ppermute | solution.py:514
  118.9 1.1 pad_maximum_fusion
  120.7 1.5 %copy.30 = bf16[4,4,96,256]{3,1,0,2:T(4,128)(2,1)} copy(bf16[4,4,96,256]{3,2,0,1:T(8,128)(2,1)S(1)} %bitcast.37) | data formatting | bytes 1572864 | tf_op jit(solution)/shard_map/transpose | solution.py:526
  122.2 2.3 %reshape.54 = bf16[16,96,256]{2,0,1:T(8,128)(2,1)} reshape(bf16[4,4,96,256]{3,1,0,2:T(4,128)(2,1)} %copy.30) | data formatting | bytes 1572864 | tf_op jit(solution)/shard_map/reshape | solution.py:526
  124.5 0.9 convert_reduce_fusion
  125.5 1.6 %collective-permute-start.6 = (f32[32,64]{1,0:T(8,128)S(1)}, f32[32,64]{1,0:T(8,128)S(1)}, u32[]{:S(2)}, u32[]{:S(2)}) collective-permute-start(f32[32,64]{1,0:T(8,128)S(1)} %reduce_sum.19), channel_id=1, source_target_pairs={{0,1},{1,0},{2,3},{3,2},{4,5},{5,4},{6,7},{7,6},{8,9},{9,8},{10,11... | collective-permute-start | bytes 24584 | tf_op jit(solution)/shard_map/ppermute | solution.py:640
  127.9 1.2 slice_convert_fusion
  129.1 1.6 %copy.31 = f32[8,8,16,256]{3,1,2,0:T(8,128)} copy(f32[8,8,16,256]{3,2,1,0:T(8,128)S(1)} %bitcast.35) | data formatting | bytes 2097152
  132.5 3.2 %shard_map.157 = bf16[128,4096]{1,0:T(8,128)(2,1)} custom-call(bf16[16,256,128]{2,1,0:T(8,128)(2,1)S(1)} %copy-done.7, bf16[128,4096]{1,0:T(8,128)(2,1)S(1)} %copy-done.1), custom_call_target="tpu_custom_call" | custom-call | flops 524288 | bytes 3145728 | tf_op jit(solution)/shard_map/pallas_call | solution.py:496
  135.8 1.2 copy-done.5
  137.0 2.9 %shard_map.159 = (bf16[128,4096]{1,0:T(8,128)(2,1)}, bf16[128,4096]{1,0:T(8,128)(2,1)}) custom-call(bf16[16,256,128]{2,1,0:T(8,128)(2,1)} %all-to-all-done.3.refs_0_, bf16[128,4096]{1,0:T(8,128)(2,1)S(1)} %copy-done.5, bf16[128,4096]{1,0:T(8,128)(2,1)S(1)} %copy-done.3), custom_call_target="tpu_custom_call" | custom-call | flops 524288 | bytes 5242880 | tf_op jit(solution)/shard_map/pallas_call | solution.py:496
  (51 shorter events, 12.5 us)
Async XLA Ops:
  0.6 12.2 %copy-start = (f32[64,4096]{1,0:T(8,128)S(1)}, f32[64,4096]{1,0:T(8,128)}, u32[]{:S(2)}) copy-start(f32[64,4096]{1,0:T(8,128)} %param.15) | copy-start | bytes 3145732
  0.6 29.1 %copy-start.1 = (bf16[128,4096]{1,0:T(8,128)(2,1)S(1)}, bf16[128,4096]{1,0:T(8,128)(2,1)}, u32[]{:S(2)}) copy-start(bf16[128,4096]{1,0:T(8,128)(2,1)} %refs_1_.2) | copy-start | bytes 3145732
  0.7 1.4 copy-start.2
  2.0 1.2 copy-start.4
  3.3 12.6 %copy-start.10 = (f32[32,64]{1,0:T(8,128)S(1)}, f32[32,64]{1,0:T(8,128)}, u32[]{:S(2)}) copy-start(f32[32,64]{1,0:T(8,128)} %param.14) | copy-start | bytes 24580
  3.3 26.5 %copy-start.8 = (bf16[128,4096]{1,0:T(8,128)(2,1)S(1)}, bf16[128,4096]{1,0:T(8,128)(2,1)}, u32[]{:S(2)}) copy-start(bf16[128,4096]{1,0:T(8,128)(2,1)} %right_any.3) | copy-start | bytes 3145732
  5.4 30.5 %all-to-all-start = ((bf16[16,256,128]{2,1,0:T(8,128)(2,1)}), bf16[16,256,128]{2,1,0:T(8,128)(2,1)}, u32[]{:S(2)}, u32[]{:S(2)}) async-start(bf16[16,256,128]{2,1,0:T(8,128)(2,1)} %shard_map.153), calls=%async_computation | async-start | bytes 2097152 | tf_op jit(solution)/shard_map/all_to_all | solution.py:538
  35.9 29.8 %all-to-all-start.2 = ((bf16[16,256,128]{2,1,0:T(8,128)(2,1)}), bf16[16,256,128]{2,1,0:T(8,128)(2,1)S(1)}, u32[]{:S(2)}, u32[]{:S(2)}) async-start(bf16[16,256,128]{2,1,0:T(8,128)(2,1)} %shard_map.154), calls=%async_computation.2 | async-start | bytes 2097152 | tf_op jit(solution)/shard_map/all_to_all | solution.py:538
  65.7 1.0 copy-start.9
  66.6 40.2 %all-to-all-start.1 = ((bf16[16,256,128]{2,1,0:T(8,128)(2,1)}), bf16[16,256,128]{2,1,0:T(8,128)(2,1)S(1)}, u32[]{:S(2)}, u32[]{:S(2)}) async-start(bf16[16,256,128]{2,1,0:T(8,128)(2,1)} %get-tuple-element.27), calls=%async_computation.1 | async-start | bytes 2097152 | tf_op jit(solution)/shard_map/all_to_all | solution.py:538
  94.1 6.0 %collective-permute-start.2 = (bf16[96,256]{1,0:T(8,128)(2,1)S(1)}, bf16[96,256]{1,0:T(8,128)(2,1)S(1)}, u32[]{:S(2)}, u32[]{:S(2)}) collective-permute-start(bf16[96,256]{1,0:T(8,128)(2,1)S(1)} %constant_dynamic-update-slice_fusion), channel_id=1, source_target_pairs={{0,24},{2,26},{4,28},{6,30},{8,16},{10,18},{12,20},{14,22},{16,8},... | collective-permute-start | bytes 147464 | tf_op jit(solution)/shard_map/ppermute | solution.py:514
  97.8 6.4 %collective-permute-start.1 = (bf16[96,256]{1,0:T(8,128)(2,1)S(1)}, bf16[96,256]{1,0:T(8,128)(2,1)S(1)}, u32[]{:S(2)}, u32[]{:S(2)}) collective-permute-start(bf16[96,256]{1,0:T(8,128)(2,1)S(1)} %constant_dynamic-update-slice_fusion), channel_id=1, source_target_pairs={{0,16},{2,18},{4,20},{6,22},{8,24},{10,26},{12,28},{14,30},{16,0},... | collective-permute-start | bytes 147464 | tf_op jit(solution)/shard_map/ppermute | solution.py:514
  97.8 6.4 %collective-permute-start = (bf16[96,256]{1,0:T(8,128)(2,1)S(1)}, bf16[96,256]{1,0:T(8,128)(2,1)S(1)}, u32[]{:S(2)}, u32[]{:S(2)}) collective-permute-start(bf16[96,256]{1,0:T(8,128)(2,1)S(1)} %constant_dynamic-update-slice_fusion), channel_id=1, source_target_pairs={{0,8},{2,10},{4,12},{6,14},{8,0},{10,2},{12,4},{14,6},{16,24},{18,... | collective-permute-start | bytes 147464 | tf_op jit(solution)/shard_map/ppermute | solution.py:514
  105.0 7.4 %collective-permute-start.5 = (bf16[4,96,256]{2,1,0:T(8,128)(2,1)}, bf16[4,96,256]{2,1,0:T(8,128)(2,1)S(1)}, u32[]{:S(2)}, u32[]{:S(2)}) collective-permute-start(bf16[4,96,256]{2,1,0:T(8,128)(2,1)} %get-tuple-element.42), channel_id=1, source_target_pairs={{0,6},{2,4},{4,2},{6,0},{8,14},{10,12},{12,10},{14,8},{16,22},{18,... | collective-permute-start | bytes 589832 | tf_op jit(solution)/shard_map/ppermute | solution.py:514
  105.7 13.1 %collective-permute-start.4 = (bf16[4,96,256]{2,1,0:T(8,128)(2,1)}, bf16[4,96,256]{2,1,0:T(8,128)(2,1)}, u32[]{:S(2)}, u32[]{:S(2)}) collective-permute-start(bf16[4,96,256]{2,1,0:T(8,128)(2,1)} %get-tuple-element.42), channel_id=1, source_target_pairs={{0,4},{2,6},{4,0},{6,2},{8,12},{10,14},{12,8},{14,10},{16,20},{18,... | collective-permute-start | bytes 589832 | tf_op jit(solution)/shard_map/ppermute | solution.py:514
  106.5 12.4 %collective-permute-start.3 = (bf16[4,96,256]{2,1,0:T(8,128)(2,1)}, bf16[4,96,256]{2,1,0:T(8,128)(2,1)}, u32[]{:S(2)}, u32[]{:S(2)}) collective-permute-start(bf16[4,96,256]{2,1,0:T(8,128)(2,1)} %get-tuple-element.42), channel_id=1, source_target_pairs={{0,2},{2,0},{4,6},{6,4},{8,10},{10,8},{12,14},{14,12},{16,18},{18,... | collective-permute-start | bytes 589832 | tf_op jit(solution)/shard_map/ppermute | solution.py:514
  106.9 13.6 %copy-start.6 = (bf16[16,256,128]{2,1,0:T(8,128)(2,1)}, bf16[16,256,128]{2,1,0:T(8,128)(2,1)S(1)}, u32[]{:S(2)}) copy-start(bf16[16,256,128]{2,1,0:T(8,128)(2,1)S(1)} %all-to-all-done.1.refs_0_) | copy-start | bytes 3145732
  106.9 28.9 %all-to-all-start.3 = ((bf16[16,256,128]{2,1,0:T(8,128)(2,1)}), bf16[16,256,128]{2,1,0:T(8,128)(2,1)}, u32[]{:S(2)}, u32[]{:S(2)}) async-start(bf16[16,256,128]{2,1,0:T(8,128)(2,1)} %get-tuple-element.36), calls=%async_computation.3 | async-start | bytes 2097152 | tf_op jit(solution)/shard_map/all_to_all | solution.py:538
  122.2 13.6 %copy-start.3 = (bf16[128,4096]{1,0:T(8,128)(2,1)S(1)}, bf16[128,4096]{1,0:T(8,128)(2,1)}, u32[]{:S(2)}) copy-start(bf16[128,4096]{1,0:T(8,128)(2,1)} %refs_2_.1) | copy-start | bytes 3145732
  125.5 6.9 %copy-start.7 = (bf16[16,256,128]{2,1,0:T(8,128)(2,1)S(1)}, bf16[16,256,128]{2,1,0:T(8,128)(2,1)}, u32[]{:S(2)}) copy-start(bf16[16,256,128]{2,1,0:T(8,128)(2,1)} %copy-done.6) | copy-start | bytes 3145732
  125.5 6.3 %collective-permute-start.6 = (f32[32,64]{1,0:T(8,128)S(1)}, f32[32,64]{1,0:T(8,128)S(1)}, u32[]{:S(2)}, u32[]{:S(2)}) collective-permute-start(f32[32,64]{1,0:T(8,128)S(1)} %reduce_sum.19), channel_id=1, source_target_pairs={{0,1},{1,0},{2,3},{3,2},{4,5},{5,4},{6,7},{7,6},{8,9},{9,8},{10,11... | collective-permute-start | bytes 24584 | tf_op jit(solution)/shard_map/ppermute | solution.py:640
  135.7 1.2 copy-start.5

commit v2 on v1

--- a/solution.py
+++ b/solution.py
@@ -459,7 +459,7 @@
             pltpu.VMEM(out.shape, jnp.bfloat16),
             pltpu.SemaphoreType.DMA((3 * count // group,)),
         ],
-        compiler_params=params(16),
+        compiler_params=params(),
         cost_estimate=estimate(rows * columns, rows * columns * 6),
     )(left, right)
 
@@ -501,7 +501,7 @@
         scratch_shapes=[pltpu.VMEM(back.shape, jnp.bfloat16)]
         + [wide] * (2 * len(factors))
         + [pltpu.SemaphoreType.DMA((copies,))],
-        compiler_params=params(16),
+        compiler_params=params(),
         cost_estimate=estimate(rows * columns, rows * columns * (2 + 4 * len(factors))),
     )(back, *factors)
 

time: 141 us -> 138 us (0.979)
  local copies, waits for them, and re-layouts: 17.7 us -> 12.6 us
    unnamed x26 -> x16, local copies, waits for them, and re-layouts: 8.4 us -> 5.57 us
  transfers between devices with their start and end apart: 11 -> 11, of which waited for: 6 -> 7; matrix products, arithmetic and copies ran while one was open for 17% -> 16% of each run, Pallas kernels for 34% -> 35%
where the time goes in v2:
time: 138 us; the launch traced here: 136 us
  Pallas kernels  52.9 us (38%)
  starting transfers between devices  32.7 us (24%)
  waiting for transfers between devices  25.8 us (19%)
  local copies, waits for them, and re-layouts  12.6 us (9%)
  other arithmetic  7.3 us (5%)
  matrix products  3.43 us (2%)
    all_to_all x4, starting transfers between devices, exchange(): lax.all_to_all(values, 'seq', split_axis=0, concat_axis=0, tiled=True)  24.9 us
    pallas_call x1, Pallas kernels, per_device(): pl.pallas_call(grad_kernel, in_specs=[in_vmem, in_vmem, anywhere, anywher...  19 us
    ppermute x6, waiting for transfers between devices, swaps(): received.append(lax.ppermute(held, 'seq', pairs))  14.3 us
    pallas_call x1, Pallas kernels, per_device(): pl.pallas_call(conv_kernel, in_specs=[in_vmem, anywhere, in_vmem, in_vmem...  12.9 us
    all_to_all x4, waiting for transfers between devices, exchange(): lax.all_to_all(values, 'seq', split_axis=0, concat_axis=0, tiled=True)  11.5 us
    pallas_call x1, Pallas kernels, per_device(): pl.pallas_call(filter_kernel, in_specs=[in_vmem] * 5, out_specs=[in_vmem,...  9.7 us
    ppermute x6, starting transfers between devices, swaps(): received.append(lax.ppermute(held, 'seq', pairs))  6.25 us
    pallas_call x2, Pallas kernels, ungate(): pl.pallas_call(functools.partial(ungate_kernel, group, len(factors)), in_...  5.8 us
  transfers between devices with their start and end apart: 11, of which 7 were waited for; matrix products, arithmetic and copies ran while one was open for 16% of the time, Pallas kernels for 35%

profile of v2, /device:TPU:0, one launch (start us, length us, event | category | flops | bytes accessed | tf_op | source)
XLA Modules:
  0.0 135.8 jit_solution(18203622710720929097)
XLA Ops:
  0.7 2.8 %shard_map.153 = bf16[16,256,128]{2,1,0:T(8,128)(2,1)} custom-call(bf16[128,4096]{1,0:T(8,128)(2,1)} %refs_2_.1, bf16[128,4096]{1,0:T(8,128)(2,1)} %refs_1_.3), custom_call_target="tpu_custom_call" | custom-call | flops 524288 | bytes 3145728 | tf_op jit(solution)/shard_map/pallas_call | solution.py:451
  3.5 7.4 %all-to-all-start = ((bf16[16,256,128]{2,1,0:T(8,128)(2,1)}), bf16[16,256,128]{2,1,0:T(8,128)(2,1)S(1)}, u32[]{:S(2)}, u32[]{:S(2)}) async-start(bf16[16,256,128]{2,1,0:T(8,128)(2,1)} %shard_map.153), calls=%async_computation | async-start | bytes 2097152 | tf_op jit(solution)/shard_map/all_to_all | solution.py:538
  12.4 0.8 copy.26.decay_ref
  13.8 3.4 %cosine_bitcast_fusion = (f32[64,2048]{1,0:T(8,128)}, f32[64,2048]{1,0:T(8,128)}) fusion(f32[32,64]{1,0:T(8,128)S(1)} %copy-done.5, f32[16,2048]{1,0:T(8,128)S(1)} %get-tuple-element.46, f32[16,2048]{1,0:T(8,128)S(1)} %get-tuple-element.45), kind=kOutput, calls=%fused_computation.6 | convolution fusion | flops 50397184 | bytes 1318912 | tf_op jit(solution)/shard_map/dot_general | solution.py:546
  17.3 9.7 %shard_map.155 = (f32[256,2048]{1,0:T(8,128)}, f32[16,256,256]{2,1,0:T(8,128)}) custom-call(f32[256,64]{1,0:T(8,128)} %copy.25.w_t_ref, f32[64,2048]{1,0:T(8,128)} %get-tuple-element.40.hidden_ref, f32[256,1]{1,0:T(8,128)} %copy.26.decay_ref, f32[2,256,256]{2,1,0:T(8,128)} %constant.63.clone.table_ref, f32[16,256]{1,0:T(8,128)} %constant.64.clone.twiddle_ref), custom_call_target="tpu_custom_call" | custom-call | flops 1000 | bytes 1000 | tf_op jit(solution)/shard_map/pallas_call | solution.py:563
  27.7 2.7 %shard_map.154 = bf16[16,256,128]{2,1,0:T(8,128)(2,1)} custom-call(bf16[128,4096]{1,0:T(8,128)(2,1)} %refs_1_.2, bf16[128,4096]{1,0:T(8,128)(2,1)} %right_any.3), custom_call_target="tpu_custom_call" | custom-call | flops 524288 | bytes 3145728 | tf_op jit(solution)/shard_map/pallas_call | solution.py:451
  31.8 2.0 %all-to-all-done.x_ref = bf16[16,256,128]{2,1,0:T(8,128)(2,1)S(1)} async-done(((bf16[16,256,128]{2,1,0:T(8,128)(2,1)}), bf16[16,256,128]{2,1,0:T(8,128)(2,1)S(1)}, u32[]{:S(2)}, u32[]{:S(2)}) %all-to-all-start) | async-done | bytes 1048608 | tf_op jit(solution)/shard_map/all_to_all | solution.py:538
  33.8 6.9 %all-to-all-start.2 = ((bf16[16,256,128]{2,1,0:T(8,128)(2,1)}), bf16[16,256,128]{2,1,0:T(8,128)(2,1)S(1)}, u32[]{:S(2)}, u32[]{:S(2)}) async-start(bf16[16,256,128]{2,1,0:T(8,128)(2,1)} %shard_map.154), calls=%async_computation.2 | async-start | bytes 2097152 | tf_op jit(solution)/shard_map/all_to_all | solution.py:538
  40.7 0.8 copy.27.skip_ref
  41.5 12.9 %shard_map.156 = (bf16[16,256,128]{2,1,0:T(8,128)(2,1)}, f32[16,256,256]{2,1,0:T(8,128)}) custom-call(bf16[16,256,128]{2,1,0:T(8,128)(2,1)} %copy-done.3, f32[16,256,256]{2,1,0:T(8,128)} %get-tuple-element.25.h_any, f32[2,256,256]{2,1,0:T(8,128)} %constant.63.clone.table_ref, f32[16,256]{1,0:T(8,128)} %constant.64.clone.twiddle_ref, f32[256,1]{1,0:T(8,128)} %copy.27.skip_ref), custom_call_target="tpu_custom_call" | custom-call | flops 3221225472 | bytes 10485760 | tf_op jit(solution)/shard_map/pallas_call | solution.py:582
  54.4 9.2 %all-to-all-done.2.g_ref = bf16[16,256,128]{2,1,0:T(8,128)(2,1)S(1)} async-done(((bf16[16,256,128]{2,1,0:T(8,128)(2,1)}), bf16[16,256,128]{2,1,0:T(8,128)(2,1)S(1)}, u32[]{:S(2)}, u32[]{:S(2)}) %all-to-all-start.2) | async-done | bytes 1048608 | tf_op jit(solution)/shard_map/all_to_all | solution.py:538
  63.6 1.0 copy-done.4
  64.6 6.9 %all-to-all-start.1 = ((bf16[16,256,128]{2,1,0:T(8,128)(2,1)}), bf16[16,256,128]{2,1,0:T(8,128)(2,1)S(1)}, u32[]{:S(2)}, u32[]{:S(2)}) async-start(bf16[16,256,128]{2,1,0:T(8,128)(2,1)} %get-tuple-element.27), calls=%async_computation.1 | async-start | bytes 2097152 | tf_op jit(solution)/shard_map/all_to_all | solution.py:538
  71.5 19.0 %shard_map.158 = (bf16[16,256,128]{2,1,0:T(8,128)(2,1)}, bf16[80,256]{1,0:T(8,128)(2,1)}, bf16[64,64]{1,0:T(8,128)(2,1)}) custom-call(bf16[16,256,128]{2,1,0:T(8,128)(2,1)} %copy-done.3, bf16[16,256,128]{2,1,0:T(8,128)(2,1)} %copy-done.4, f32[16,256,256]{2,1,0:T(8,128)} %get-tuple-element.29.x_any, f32[16,256,256]{2,1,0:T(8,128)} %get-tuple-element.25.h_any, ...), custom_call_target="tpu_custom_call" | custom-call | flops 4831838208 | bytes 10485760 | tf_op jit(solution)/shard_map/pallas_call | solution.py:593
  90.5 0.8 reshape.51
  91.3 0.8 constant_dynamic-update-slice_fusion.1
  92.1 3.7 %collective-permute-start.2 = (bf16[96,256]{1,0:T(8,128)(2,1)S(1)}, bf16[96,256]{1,0:T(8,128)(2,1)S(1)}, u32[]{:S(2)}, u32[]{:S(2)}) collective-permute-start(bf16[96,256]{1,0:T(8,128)(2,1)S(1)} %constant_dynamic-update-slice_fusion), channel_id=1, source_target_pairs={{0,24},{2,26},{4,28},{6,30},{8,16},{10,18},{12,20},{14,22},{16,8},... | collective-permute-start | bytes 147464 | tf_op jit(solution)/shard_map/ppermute | solution.py:514
  96.5 1.6 %collective-permute-done.2 = bf16[96,256]{1,0:T(8,128)(2,1)S(1)} collective-permute-done((bf16[96,256]{1,0:T(8,128)(2,1)S(1)}, bf16[96,256]{1,0:T(8,128)(2,1)S(1)}, u32[]{:S(2)}, u32[]{:S(2)}) %collective-permute-start.2) | collective-permute-done | bytes 49184 | tf_op jit(solution)/shard_map/ppermute | solution.py:514
  98.1 4.2 %collective-permute-done.1 = bf16[96,256]{1,0:T(8,128)(2,1)S(1)} collective-permute-done((bf16[96,256]{1,0:T(8,128)(2,1)S(1)}, bf16[96,256]{1,0:T(8,128)(2,1)S(1)}, u32[]{:S(2)}, u32[]{:S(2)}) %collective-permute-start.1) | collective-permute-done | bytes 49184 | tf_op jit(solution)/shard_map/ppermute | solution.py:514
  103.7 0.8 collective-permute-start.4
  104.8 3.7 %all-to-all-start.3 = ((bf16[16,256,128]{2,1,0:T(8,128)(2,1)}), bf16[16,256,128]{2,1,0:T(8,128)(2,1)S(1)}, u32[]{:S(2)}, u32[]{:S(2)}) async-start(bf16[16,256,128]{2,1,0:T(8,128)(2,1)} %get-tuple-element.36), calls=%async_computation.3 | async-start | bytes 2097152 | tf_op jit(solution)/shard_map/all_to_all | solution.py:538
  108.6 1.8 %collective-permute-done.5 = bf16[4,96,256]{2,1,0:T(8,128)(2,1)S(1)} collective-permute-done((bf16[4,96,256]{2,1,0:T(8,128)(2,1)}, bf16[4,96,256]{2,1,0:T(8,128)(2,1)S(1)}, u32[]{:S(2)}, u32[]{:S(2)}) %collective-permute-start.5) | collective-permute-done | bytes 196640 | tf_op jit(solution)/shard_map/ppermute | solution.py:514
  110.3 6.8 %collective-permute-done.4 = bf16[4,96,256]{2,1,0:T(8,128)(2,1)} collective-permute-done((bf16[4,96,256]{2,1,0:T(8,128)(2,1)}, bf16[4,96,256]{2,1,0:T(8,128)(2,1)}, u32[]{:S(2)}, u32[]{:S(2)}) %collective-permute-start.4) | collective-permute-done | bytes 196640 | tf_op jit(solution)/shard_map/ppermute | solution.py:514
  117.1 1.1 pad_maximum_fusion
  119.5 1.1 reshape.54
  120.6 0.9 convert_reduce_fusion
  121.6 1.6 %collective-permute-start.6 = (f32[32,64]{1,0:T(8,128)S(1)}, f32[32,64]{1,0:T(8,128)S(1)}, u32[]{:S(2)}, u32[]{:S(2)}) collective-permute-start(f32[32,64]{1,0:T(8,128)S(1)} %reduce_sum.19), channel_id=1, source_target_pairs={{0,1},{1,0},{2,3},{3,2},{4,5},{5,4},{6,7},{7,6},{8,9},{9,8},{10,11... | collective-permute-start | bytes 24584 | tf_op jit(solution)/shard_map/ppermute | solution.py:640
  123.9 1.2 slice_convert_fusion
  125.1 1.6 %copy.31 = f32[8,8,16,256]{3,1,2,0:T(8,128)} copy(f32[8,8,16,256]{3,2,1,0:T(8,128)S(1)} %bitcast.35) | data formatting | bytes 2097152
  128.5 2.7 %shard_map.157 = bf16[128,4096]{1,0:T(8,128)(2,1)} custom-call(bf16[16,256,128]{2,1,0:T(8,128)(2,1)} %copy-done.1, bf16[128,4096]{1,0:T(8,128)(2,1)} %refs_1_.2), custom_call_target="tpu_custom_call" | custom-call | flops 524288 | bytes 3145728 | tf_op jit(solution)/shard_map/pallas_call | solution.py:496
  131.5 1.0 copy-done.2
  132.5 3.1 %shard_map.159 = (bf16[128,4096]{1,0:T(8,128)(2,1)}, bf16[128,4096]{1,0:T(8,128)(2,1)}) custom-call(bf16[16,256,128]{2,1,0:T(8,128)(2,1)} %copy-done.2, bf16[128,4096]{1,0:T(8,128)(2,1)} %refs_1_.3, bf16[128,4096]{1,0:T(8,128)(2,1)} %refs_2_.1), custom_call_target="tpu_custom_call" | custom-call | flops 524288 | bytes 5242880 | tf_op jit(solution)/shard_map/pallas_call | solution.py:496
  (41 shorter events, 10.9 us)
Async XLA Ops:
  0.6 10.3 %copy-start = (f32[64,4096]{1,0:T(8,128)S(1)}, f32[64,4096]{1,0:T(8,128)}, u32[]{:S(2)}) copy-start(f32[64,4096]{1,0:T(8,128)} %param.15) | copy-start | bytes 3145732
  0.6 13.2 %copy-start.5 = (f32[32,64]{1,0:T(8,128)S(1)}, f32[32,64]{1,0:T(8,128)}, u32[]{:S(2)}) copy-start(f32[32,64]{1,0:T(8,128)} %param.14) | copy-start | bytes 24580
  3.5 30.3 %all-to-all-start = ((bf16[16,256,128]{2,1,0:T(8,128)(2,1)}), bf16[16,256,128]{2,1,0:T(8,128)(2,1)S(1)}, u32[]{:S(2)}, u32[]{:S(2)}) async-start(bf16[16,256,128]{2,1,0:T(8,128)(2,1)} %shard_map.153), calls=%async_computation | async-start | bytes 2097152 | tf_op jit(solution)/shard_map/all_to_all | solution.py:538
  33.8 7.7 %copy-start.3 = (bf16[16,256,128]{2,1,0:T(8,128)(2,1)}, bf16[16,256,128]{2,1,0:T(8,128)(2,1)S(1)}, u32[]{:S(2)}) copy-start(bf16[16,256,128]{2,1,0:T(8,128)(2,1)S(1)} %all-to-all-done.x_ref) | copy-start | bytes 3145732
  33.8 29.8 %all-to-all-start.2 = ((bf16[16,256,128]{2,1,0:T(8,128)(2,1)}), bf16[16,256,128]{2,1,0:T(8,128)(2,1)S(1)}, u32[]{:S(2)}, u32[]{:S(2)}) async-start(bf16[16,256,128]{2,1,0:T(8,128)(2,1)} %shard_map.154), calls=%async_computation.2 | async-start | bytes 2097152 | tf_op jit(solution)/shard_map/all_to_all | solution.py:538
  63.6 1.0 copy-start.4
  64.6 40.2 %all-to-all-start.1 = ((bf16[16,256,128]{2,1,0:T(8,128)(2,1)}), bf16[16,256,128]{2,1,0:T(8,128)(2,1)S(1)}, u32[]{:S(2)}, u32[]{:S(2)}) async-start(bf16[16,256,128]{2,1,0:T(8,128)(2,1)} %get-tuple-element.27), calls=%async_computation.1 | async-start | bytes 2097152 | tf_op jit(solution)/shard_map/all_to_all | solution.py:538
  92.1 6.0 %collective-permute-start.2 = (bf16[96,256]{1,0:T(8,128)(2,1)S(1)}, bf16[96,256]{1,0:T(8,128)(2,1)S(1)}, u32[]{:S(2)}, u32[]{:S(2)}) collective-permute-start(bf16[96,256]{1,0:T(8,128)(2,1)S(1)} %constant_dynamic-update-slice_fusion), channel_id=1, source_target_pairs={{0,24},{2,26},{4,28},{6,30},{8,16},{10,18},{12,20},{14,22},{16,8},... | collective-permute-start | bytes 147464 | tf_op jit(solution)/shard_map/ppermute | solution.py:514
  95.8 6.4 %collective-permute-start.1 = (bf16[96,256]{1,0:T(8,128)(2,1)S(1)}, bf16[96,256]{1,0:T(8,128)(2,1)S(1)}, u32[]{:S(2)}, u32[]{:S(2)}) collective-permute-start(bf16[96,256]{1,0:T(8,128)(2,1)S(1)} %constant_dynamic-update-slice_fusion), channel_id=1, source_target_pairs={{0,16},{2,18},{4,20},{6,22},{8,24},{10,26},{12,28},{14,30},{16,0},... | collective-permute-start | bytes 147464 | tf_op jit(solution)/shard_map/ppermute | solution.py:514
  95.8 6.4 %collective-permute-start = (bf16[96,256]{1,0:T(8,128)(2,1)S(1)}, bf16[96,256]{1,0:T(8,128)(2,1)S(1)}, u32[]{:S(2)}, u32[]{:S(2)}) collective-permute-start(bf16[96,256]{1,0:T(8,128)(2,1)S(1)} %constant_dynamic-update-slice_fusion), channel_id=1, source_target_pairs={{0,8},{2,10},{4,12},{6,14},{8,0},{10,2},{12,4},{14,6},{16,24},{18,... | collective-permute-start | bytes 147464 | tf_op jit(solution)/shard_map/ppermute | solution.py:514
  103.0 7.4 %collective-permute-start.5 = (bf16[4,96,256]{2,1,0:T(8,128)(2,1)}, bf16[4,96,256]{2,1,0:T(8,128)(2,1)S(1)}, u32[]{:S(2)}, u32[]{:S(2)}) collective-permute-start(bf16[4,96,256]{2,1,0:T(8,128)(2,1)} %get-tuple-element.42), channel_id=1, source_target_pairs={{0,6},{2,4},{4,2},{6,0},{8,14},{10,12},{12,10},{14,8},{16,22},{18,... | collective-permute-start | bytes 589832 | tf_op jit(solution)/shard_map/ppermute | solution.py:514
  103.7 13.4 %collective-permute-start.4 = (bf16[4,96,256]{2,1,0:T(8,128)(2,1)}, bf16[4,96,256]{2,1,0:T(8,128)(2,1)}, u32[]{:S(2)}, u32[]{:S(2)}) collective-permute-start(bf16[4,96,256]{2,1,0:T(8,128)(2,1)} %get-tuple-element.42), channel_id=1, source_target_pairs={{0,4},{2,6},{4,0},{6,2},{8,12},{10,14},{12,8},{14,10},{16,20},{18,... | collective-permute-start | bytes 589832 | tf_op jit(solution)/shard_map/ppermute | solution.py:514
  104.5 12.6 %collective-permute-start.3 = (bf16[4,96,256]{2,1,0:T(8,128)(2,1)}, bf16[4,96,256]{2,1,0:T(8,128)(2,1)}, u32[]{:S(2)}, u32[]{:S(2)}) collective-permute-start(bf16[4,96,256]{2,1,0:T(8,128)(2,1)} %get-tuple-element.42), channel_id=1, source_target_pairs={{0,2},{2,0},{4,6},{6,4},{8,10},{10,8},{12,14},{14,12},{16,18},{18,... | collective-permute-start | bytes 589832 | tf_op jit(solution)/shard_map/ppermute | solution.py:514
  104.8 13.9 %copy-start.1 = (bf16[16,256,128]{2,1,0:T(8,128)(2,1)}, bf16[16,256,128]{2,1,0:T(8,128)(2,1)S(1)}, u32[]{:S(2)}) copy-start(bf16[16,256,128]{2,1,0:T(8,128)(2,1)S(1)} %all-to-all-done.1.refs_0_) | copy-start | bytes 3145732
  104.8 26.7 %all-to-all-start.3 = ((bf16[16,256,128]{2,1,0:T(8,128)(2,1)}), bf16[16,256,128]{2,1,0:T(8,128)(2,1)S(1)}, u32[]{:S(2)}, u32[]{:S(2)}) async-start(bf16[16,256,128]{2,1,0:T(8,128)(2,1)} %get-tuple-element.36), calls=%async_computation.3 | async-start | bytes 2097152 | tf_op jit(solution)/shard_map/all_to_all | solution.py:538
  121.6 6.3 %collective-permute-start.6 = (f32[32,64]{1,0:T(8,128)S(1)}, f32[32,64]{1,0:T(8,128)S(1)}, u32[]{:S(2)}, u32[]{:S(2)}) collective-permute-start(f32[32,64]{1,0:T(8,128)S(1)} %reduce_sum.19), channel_id=1, source_target_pairs={{0,1},{1,0},{2,3},{3,2},{4,5},{5,4},{6,7},{7,6},{8,9},{9,8},{10,11... | collective-permute-start | bytes 24584 | tf_op jit(solution)/shard_map/ppermute | solution.py:640
  131.5 1.0 copy-start.2

commit v3 on v2

--- a/solution.py
+++ b/solution.py
@@ -367,7 +367,13 @@
         hidden_part = dot_pairs(w_pair, raw_pair, 0) * cosine_ref[:, columns]
         first += dot_pairs(split_bf16(positional_ref[:, columns]), split_bf16(hidden_part), 1)
 
-    first_ref[:band_total, :], first_ref[band_total:, :] = split_bf16(first * scale)
+    first_pair = split_bf16(first * scale)
+    first_ref[:band_total, :], first_ref[band_total:, :] = first_pair
+    rows = small_ref.shape[0] - hidden_count - 16
+    if rows > 0:
+        stacked = jnp.concatenate([part.astype(jnp.float32) for part in first_pair], axis=0)
+        pieces = [stacked[at : at + rows] for at in range(0, 2 * band_total, rows)]
+        small_ref[hidden_count + 16 :, :] = jnp.concatenate(pieces, axis=1).astype(jnp.bfloat16)
     small_ref[:hidden_count, :] = (second * scale).astype(jnp.bfloat16)
     place = lax.broadcasted_iota(jnp.int32, (16, width), 0)
     tail = jnp.zeros((16, width), jnp.float32)
@@ -375,10 +381,10 @@
     skip_pair = split_bf16(jnp.sum(sums[1].T, axis=0, keepdims=True) * scale)
     for at, row in enumerate(decay_pair + skip_pair):
         tail = jnp.where(place == at, row.astype(jnp.float32), tail)
-    small_ref[hidden_count:, :] = tail.astype(jnp.bfloat16)
-
-
-def params(limit=56):
+    small_ref[hidden_count : hidden_count + 16, :] = tail.astype(jnp.bfloat16)
+
+
+def params(limit=63):
     return pltpu.CompilerParams(vmem_limit_bytes=limit * MIB)
 
 
@@ -590,13 +596,16 @@
     )(gated_in, filter_spectrum, tables, twiddle, skip_mine)
     conv_back = exchange(convolved)
 
+    pieces = width // hidden_count
+    packs = width % hidden_count == 0 and 2 * band_total % (16 * pieces) == 0
+    first_count = 2 * band_total // pieces if packs else 0
     grad_gated, small, first_pair = pl.pallas_call(
         grad_kernel,
         in_specs=[in_vmem, in_vmem, anywhere, anywhere, anywhere] + [in_vmem] * 8,
         out_specs=[in_vmem, in_vmem, in_vmem],
         out_shape=[
             block_shape,
-            jax.ShapeDtypeStruct((hidden_count + 16, width), jnp.bfloat16),
+            jax.ShapeDtypeStruct((hidden_count + 16 + first_count, width), jnp.bfloat16),
             jax.ShapeDtypeStruct((2 * band_total, hidden_count), jnp.bfloat16),
         ],
         scratch_shapes=[
@@ -625,7 +634,9 @@
         cosine,
         positional,
     )
-    packed = jnp.concatenate([small, first_pair.reshape(-1, width)], axis=0)
+    packed = small
+    if not packs:
+        packed = jnp.concatenate([small, first_pair.reshape(-1, width)], axis=0)
     gathered, across = gather_all(packed, parts, seq_index, math.gcd(parts, 4))
     grad_gated, _ = lax.optimization_barrier((grad_gated, across))
     grad_back = exchange(grad_gated)
@@ -635,6 +646,8 @@
     grad_decay = (tail[:, 0] + tail[:, 1]).reshape(chan_tp)
     grad_skip = (tail[:, 2] + tail[:, 3]).reshape(chan_tp)
     first_rows = gathered[:, hidden_count + 16 :].astype(jnp.float32).sum(axis=0)
+    if packs:
+        first_rows = first_rows.reshape(first_count, pieces, hidden_count).transpose(1, 0, 2)
     grad_first = first_rows.reshape(2, band_total, hidden_count).sum(axis=0)
     if lax.axis_size("tp") == 2:
         grad_first = grad_first + lax.ppermute(grad_first, "tp", [(0, 1), (1, 0)])

time: 138 us -> 146 us (1.058)
  waiting for transfers between devices: 25.8 us -> 39.6 us
  other arithmetic: 7.3 us -> 3.69 us
  local copies, waits for them, and re-layouts: 12.6 us -> 9.92 us
    all_to_all x4, waiting for transfers between devices: 11.5 us -> 23 us  [exchange(): lax.all_to_all(values, 'seq', split_axis=0, concat_axis=0, tiled=True)]
    unnamed x16 -> x5, local copies, waits for them, and re-layouts: 5.57 us -> 2.81 us
    ppermute x6, waiting for transfers between devices: 14.3 us -> 16.6 us  [swaps(): received.append(lax.ppermute(held, 'seq', pairs))]
  transfers between devices with their start and end apart: 11 -> 11, of which waited for: 7 -> 7; matrix products, arithmetic and copies ran while one was open for 16% -> 12% of each run, Pallas kernels for 35% -> 33%
where the time goes in v3:
time: 146 us; the launch traced here: 144 us
  Pallas kernels  53.1 us (36%)
  waiting for transfers between devices  39.6 us (27%)
  starting transfers between devices  33.6 us (23%)
  local copies, waits for them, and re-layouts  9.92 us (7%)
  other arithmetic  3.69 us (3%)
  matrix products  3.46 us (2%)
    all_to_all x4, starting transfers between devices, exchange(): lax.all_to_all(values, 'seq', split_axis=0, concat_axis=0, tiled=True)  25.7 us
    all_to_all x4, waiting for transfers between devices, exchange(): lax.all_to_all(values, 'seq', split_axis=0, concat_axis=0, tiled=True)  23 us
    pallas_call x1, Pallas kernels, per_device(): pl.pallas_call(grad_kernel, in_specs=[in_vmem, in_vmem, anywhere, anywher...  19.1 us
    ppermute x6, waiting for transfers between devices, swaps(): received.append(lax.ppermute(held, 'seq', pairs))  16.6 us
    pallas_call x1, Pallas kernels, per_device(): pl.pallas_call(conv_kernel, in_specs=[in_vmem, anywhere, in_vmem, in_vmem...  12.9 us
    pallas_call x1, Pallas kernels, per_device(): pl.pallas_call(filter_kernel, in_specs=[in_vmem] * 5, out_specs=[in_vmem,...  9.8 us
    ppermute x6, starting transfers between devices, swaps(): received.append(lax.ppermute(held, 'seq', pairs))  6.38 us
    pallas_call x2, Pallas kernels, ungate(): pl.pallas_call(functools.partial(ungate_kernel, group, len(factors)), in_...  5.81 us
  transfers between devices with their start and end apart: 11, of which 7 were waited for; matrix products, arithmetic and copies ran while one was open for 12% of the time, Pallas kernels for 33%

profile of v3, /device:TPU:0, one launch (start us, length us, event | category | flops | bytes accessed | tf_op | source)
XLA Modules:
  0.0 144.4 jit_solution(6333933635871658883)
XLA Ops:
  0.6 2.7 %shard_map.153 = bf16[16,256,128]{2,1,0:T(8,128)(2,1)} custom-call(bf16[128,4096]{1,0:T(8,128)(2,1)} %refs_2_.1, bf16[128,4096]{1,0:T(8,128)(2,1)} %refs_1_.3), custom_call_target="tpu_custom_call" | custom-call | flops 524288 | bytes 3145728 | tf_op jit(solution)/shard_map/pallas_call | solution.py:457
  3.4 7.4 %all-to-all-start = ((bf16[16,256,128]{2,1,0:T(8,128)(2,1)}), bf16[16,256,128]{2,1,0:T(8,128)(2,1)}, u32[]{:S(2)}, u32[]{:S(2)}) async-start(bf16[16,256,128]{2,1,0:T(8,128)(2,1)} %shard_map.153), calls=%async_computation | async-start | bytes 2097152 | tf_op jit(solution)/shard_map/all_to_all | solution.py:544
  10.8 0.8 fusion.13
  11.7 0.8 copy.25.w_t_ref
  12.5 0.8 dynamic_slice.10
  13.2 0.8 copy.26.decay_ref
  14.6 3.5 %cosine_bitcast_fusion = (f32[64,2048]{1,0:T(8,128)}, f32[64,2048]{1,0:T(8,128)}) fusion(f32[32,64]{1,0:T(8,128)S(1)} %copy-done, f32[16,2048]{1,0:T(8,128)S(1)} %get-tuple-element.44, f32[16,2048]{1,0:T(8,128)S(1)} %get-tuple-element.43), kind=kOutput, calls=%fused_computation.6 | convolution fusion | flops 50397184 | bytes 1318912 | tf_op jit(solution)/shard_map/dot_general | solution.py:552
  18.1 9.8 %shard_map.155 = (f32[256,2048]{1,0:T(8,128)}, f32[16,256,256]{2,1,0:T(8,128)}) custom-call(f32[256,64]{1,0:T(8,128)} %copy.25.w_t_ref, f32[64,2048]{1,0:T(8,128)} %get-tuple-element.38.hidden_ref, f32[256,1]{1,0:T(8,128)} %copy.26.decay_ref, f32[2,256,256]{2,1,0:T(8,128)} %constant.63.clone.table_ref, f32[16,256]{1,0:T(8,128)} %constant.64.clone.twiddle_ref), custom_call_target="tpu_custom_call" | custom-call | flops 1000 | bytes 1000 | tf_op jit(solution)/shard_map/pallas_call | solution.py:569
  27.9 0.8 dynamic_slice.11
  28.7 2.7 %shard_map.154 = bf16[16,256,128]{2,1,0:T(8,128)(2,1)} custom-call(bf16[128,4096]{1,0:T(8,128)(2,1)} %refs_1_.2, bf16[128,4096]{1,0:T(8,128)(2,1)} %right_any.3), custom_call_target="tpu_custom_call" | custom-call | flops 524288 | bytes 3145728 | tf_op jit(solution)/shard_map/pallas_call | solution.py:457
  31.4 1.5 %constant_dynamic-slice_fusion.w_ref = f32[64,256]{1,0:T(8,128)} fusion(f32[64,4096]{1,0:T(8,128)} %param.15, s32[]{:T(128)S(6)} %select_n.58), kind=kLoop, calls=%fused_computation.31 | loop fusion | bytes 131076 | tf_op jit(solution)/shard_map/dynamic_slice | solution.py:558
  33.8 6.9 %all-to-all-start.2 = ((bf16[16,256,128]{2,1,0:T(8,128)(2,1)}), bf16[16,256,128]{2,1,0:T(8,128)(2,1)}, u32[]{:S(2)}, u32[]{:S(2)}) async-start(bf16[16,256,128]{2,1,0:T(8,128)(2,1)} %shard_map.154), calls=%async_computation.2 | async-start | bytes 2097152 | tf_op jit(solution)/shard_map/all_to_all | solution.py:544
  40.8 0.8 copy.27.skip_ref
  41.6 12.9 %shard_map.156 = (bf16[16,256,128]{2,1,0:T(8,128)(2,1)}, f32[16,256,256]{2,1,0:T(8,128)}) custom-call(bf16[16,256,128]{2,1,0:T(8,128)(2,1)} %all-to-all-done.x_ref, f32[16,256,256]{2,1,0:T(8,128)} %get-tuple-element.24.h_any, f32[2,256,256]{2,1,0:T(8,128)} %constant.63.clone.table_ref, f32[16,256]{1,0:T(8,128)} %constant.64.clone.twiddle_ref, ...), custom_call_target="tpu_custom_call" | custom-call | flops 3221225472 | bytes 10485760 | tf_op jit(solution)/shard_map/pallas_call | solution.py:588
  54.5 9.3 %all-to-all-done.2.g_ref = bf16[16,256,128]{2,1,0:T(8,128)(2,1)} async-done(((bf16[16,256,128]{2,1,0:T(8,128)(2,1)}), bf16[16,256,128]{2,1,0:T(8,128)(2,1)}, u32[]{:S(2)}, u32[]{:S(2)}) %all-to-all-start.2) | async-done | bytes 1048608 | tf_op jit(solution)/shard_map/all_to_all | solution.py:544
  63.8 6.9 %all-to-all-start.1 = ((bf16[16,256,128]{2,1,0:T(8,128)(2,1)}), bf16[16,256,128]{2,1,0:T(8,128)(2,1)}, u32[]{:S(2)}, u32[]{:S(2)}) async-start(bf16[16,256,128]{2,1,0:T(8,128)(2,1)} %get-tuple-element.26), calls=%async_computation.1 | async-start | bytes 2097152 | tf_op jit(solution)/shard_map/all_to_all | solution.py:544
  70.7 19.1 %shard_map.158 = (bf16[16,256,128]{2,1,0:T(8,128)(2,1)}, bf16[96,256]{1,0:T(8,128)(2,1)}, bf16[64,64]{1,0:T(8,128)(2,1)}) custom-call(bf16[16,256,128]{2,1,0:T(8,128)(2,1)} %all-to-all-done.x_ref, bf16[16,256,128]{2,1,0:T(8,128)(2,1)} %all-to-all-done.2.g_ref, f32[16,256,256]{2,1,0:T(8,128)} %get-tuple-element.28.x_any, ...), custom_call_target="tpu_custom_call" | custom-call | flops 4831838208 | bytes 10485760 | tf_op jit(solution)/shard_map/pallas_call | solution.py:602
  89.9 3.7 %collective-permute-start.2 = (bf16[96,256]{1,0:T(8,128)(2,1)}, bf16[96,256]{1,0:T(8,128)(2,1)S(1)}, u32[]{:S(2)}, u32[]{:S(2)}) collective-permute-start(bf16[96,256]{1,0:T(8,128)(2,1)} %get-tuple-element.33), channel_id=1, source_target_pairs={{0,24},{2,26},{4,28},{6,30},{8,16},{10,18},{12,20},{14,22},{16,8},... | collective-permute-start | bytes 147464 | tf_op jit(solution)/shard_map/ppermute | solution.py:520
  93.6 0.7 collective-permute-start
  94.3 1.8 %collective-permute-done.2 = bf16[96,256]{1,0:T(8,128)(2,1)S(1)} collective-permute-done((bf16[96,256]{1,0:T(8,128)(2,1)}, bf16[96,256]{1,0:T(8,128)(2,1)S(1)}, u32[]{:S(2)}, u32[]{:S(2)}) %collective-permute-start.2) | collective-permute-done | bytes 49184 | tf_op jit(solution)/shard_map/ppermute | solution.py:520
  96.1 5.3 %collective-permute-done.1 = bf16[96,256]{1,0:T(8,128)(2,1)S(1)} collective-permute-done((bf16[96,256]{1,0:T(8,128)(2,1)}, bf16[96,256]{1,0:T(8,128)(2,1)S(1)}, u32[]{:S(2)}, u32[]{:S(2)}) %collective-permute-start.1) | collective-permute-done | bytes 49184 | tf_op jit(solution)/shard_map/ppermute | solution.py:520
  101.4 0.8 fusion.11
  102.2 0.8 collective-permute-start.5
  103.0 0.8 collective-permute-start.4
  104.2 5.3 %collective-permute-done.5 = bf16[4,96,256]{2,1,0:T(8,128)(2,1)S(1)} collective-permute-done((bf16[4,96,256]{2,1,0:T(8,128)(2,1)S(1)}, bf16[4,96,256]{2,1,0:T(8,128)(2,1)S(1)}, u32[]{:S(2)}, u32[]{:S(2)}) %collective-permute-start.5) | collective-permute-done | bytes 196640 | tf_op jit(solution)/shard_map/ppermute | solution.py:520
  109.5 4.3 %collective-permute-done.4 = bf16[4,96,256]{2,1,0:T(8,128)(2,1)S(1)} collective-permute-done((bf16[4,96,256]{2,1,0:T(8,128)(2,1)S(1)}, bf16[4,96,256]{2,1,0:T(8,128)(2,1)S(1)}, u32[]{:S(2)}, u32[]{:S(2)}) %collective-permute-start.4) | collective-permute-done | bytes 196640 | tf_op jit(solution)/shard_map/ppermute | solution.py:520
  113.8 4.4 %all-to-all-start.3 = ((bf16[16,256,128]{2,1,0:T(8,128)(2,1)}), bf16[16,256,128]{2,1,0:T(8,128)(2,1)}, u32[]{:S(2)}, u32[]{:S(2)}) async-start(bf16[16,256,128]{2,1,0:T(8,128)(2,1)} %get-tuple-element.34), calls=%async_computation.3 | async-start | bytes 2097152 | tf_op jit(solution)/shard_map/all_to_all | solution.py:544
  119.8 1.6 %collective-permute-start.6 = (f32[32,64]{1,0:T(8,128)S(1)}, f32[32,64]{1,0:T(8,128)S(1)}, u32[]{:S(2)}, u32[]{:S(2)}) collective-permute-start(f32[32,64]{1,0:T(8,128)S(1)} %bitcast_reduce_fusion), channel_id=1, source_target_pairs={{0,1},{1,0},{2,3},{3,2},{4,5},{5,4},{6,7},{7,6},{8,9},{9,8},{10,11... | collective-permute-start | bytes 24584 | tf_op jit(solution)/shard_map/ppermute | solution.py:653
  121.6 1.6 %copy.32 = f32[8,8,16,256]{3,1,2,0:T(8,128)} copy(f32[8,8,16,256]{3,2,1,0:T(8,128)S(1)} %bitcast.39) | data formatting | bytes 2097152
  125.0 2.7 %shard_map.157 = bf16[128,4096]{1,0:T(8,128)(2,1)} custom-call(bf16[16,256,128]{2,1,0:T(8,128)(2,1)} %all-to-all-done.1.refs_0_, bf16[128,4096]{1,0:T(8,128)(2,1)} %refs_1_.2), custom_call_target="tpu_custom_call" | custom-call | flops 524288 | bytes 3145728 | tf_op jit(solution)/shard_map/pallas_call | solution.py:502
  127.7 13.4 %all-to-all-done.3.refs_0_ = bf16[16,256,128]{2,1,0:T(8,128)(2,1)} async-done(((bf16[16,256,128]{2,1,0:T(8,128)(2,1)}), bf16[16,256,128]{2,1,0:T(8,128)(2,1)}, u32[]{:S(2)}, u32[]{:S(2)}) %all-to-all-start.3) | async-done | bytes 1048608 | tf_op jit(solution)/shard_map/all_to_all | solution.py:544
  141.1 3.1 %shard_map.159 = (bf16[128,4096]{1,0:T(8,128)(2,1)}, bf16[128,4096]{1,0:T(8,128)(2,1)}) custom-call(bf16[16,256,128]{2,1,0:T(8,128)(2,1)} %all-to-all-done.3.refs_0_, bf16[128,4096]{1,0:T(8,128)(2,1)} %refs_1_.3, bf16[128,4096]{1,0:T(8,128)(2,1)} %refs_2_.1), custom_call_target="tpu_custom_call" | custom-call | flops 524288 | bytes 5242880 | tf_op jit(solution)/shard_map/pallas_call | solution.py:502
  (29 shorter events, 5.5 us)
Async XLA Ops:
  0.6 14.0 %copy-start = (f32[32,64]{1,0:T(8,128)S(1)}, f32[32,64]{1,0:T(8,128)}, u32[]{:S(2)}) copy-start(f32[32,64]{1,0:T(8,128)} %param.14) | copy-start | bytes 24580
  3.4 30.5 %all-to-all-start = ((bf16[16,256,128]{2,1,0:T(8,128)(2,1)}), bf16[16,256,128]{2,1,0:T(8,128)(2,1)}, u32[]{:S(2)}, u32[]{:S(2)}) async-start(bf16[16,256,128]{2,1,0:T(8,128)(2,1)} %shard_map.153), calls=%async_computation | async-start | bytes 2097152 | tf_op jit(solution)/shard_map/all_to_all | solution.py:544
  33.8 29.9 %all-to-all-start.2 = ((bf16[16,256,128]{2,1,0:T(8,128)(2,1)}), bf16[16,256,128]{2,1,0:T(8,128)(2,1)}, u32[]{:S(2)}, u32[]{:S(2)}) async-start(bf16[16,256,128]{2,1,0:T(8,128)(2,1)} %shard_map.154), calls=%async_computation.2 | async-start | bytes 2097152 | tf_op jit(solution)/shard_map/all_to_all | solution.py:544
  63.8 50.1 %all-to-all-start.1 = ((bf16[16,256,128]{2,1,0:T(8,128)(2,1)}), bf16[16,256,128]{2,1,0:T(8,128)(2,1)}, u32[]{:S(2)}, u32[]{:S(2)}) async-start(bf16[16,256,128]{2,1,0:T(8,128)(2,1)} %get-tuple-element.26), calls=%async_computation.1 | async-start | bytes 2097152 | tf_op jit(solution)/shard_map/all_to_all | solution.py:544
  89.9 6.2 %collective-permute-start.2 = (bf16[96,256]{1,0:T(8,128)(2,1)}, bf16[96,256]{1,0:T(8,128)(2,1)S(1)}, u32[]{:S(2)}, u32[]{:S(2)}) collective-permute-start(bf16[96,256]{1,0:T(8,128)(2,1)} %get-tuple-element.33), channel_id=1, source_target_pairs={{0,24},{2,26},{4,28},{6,30},{8,16},{10,18},{12,20},{14,22},{16,8},... | collective-permute-start | bytes 147464 | tf_op jit(solution)/shard_map/ppermute | solution.py:520
  93.6 7.8 %collective-permute-start.1 = (bf16[96,256]{1,0:T(8,128)(2,1)}, bf16[96,256]{1,0:T(8,128)(2,1)S(1)}, u32[]{:S(2)}, u32[]{:S(2)}) collective-permute-start(bf16[96,256]{1,0:T(8,128)(2,1)} %get-tuple-element.33), channel_id=1, source_target_pairs={{0,16},{2,18},{4,20},{6,22},{8,24},{10,26},{12,28},{14,30},{16,0},... | collective-permute-start | bytes 147464 | tf_op jit(solution)/shard_map/ppermute | solution.py:520
  93.6 7.8 %collective-permute-start = (bf16[96,256]{1,0:T(8,128)(2,1)}, bf16[96,256]{1,0:T(8,128)(2,1)S(1)}, u32[]{:S(2)}, u32[]{:S(2)}) collective-permute-start(bf16[96,256]{1,0:T(8,128)(2,1)} %get-tuple-element.33), channel_id=1, source_target_pairs={{0,8},{2,10},{4,12},{6,14},{8,0},{10,2},{12,4},{14,6},{16,24},{18,... | collective-permute-start | bytes 147464 | tf_op jit(solution)/shard_map/ppermute | solution.py:520
  102.2 7.2 %collective-permute-start.5 = (bf16[4,96,256]{2,1,0:T(8,128)(2,1)S(1)}, bf16[4,96,256]{2,1,0:T(8,128)(2,1)S(1)}, u32[]{:S(2)}, u32[]{:S(2)}) collective-permute-start(bf16[4,96,256]{2,1,0:T(8,128)(2,1)S(1)} %get-tuple-element.40), channel_id=1, source_target_pairs={{0,6},{2,4},{4,2},{6,0},{8,14},{10,12},{12,10},{14,8},{16,22},{18,... | collective-permute-start | bytes 589832 | tf_op jit(solution)/shard_map/ppermute | solution.py:520
  103.0 10.7 %collective-permute-start.4 = (bf16[4,96,256]{2,1,0:T(8,128)(2,1)S(1)}, bf16[4,96,256]{2,1,0:T(8,128)(2,1)S(1)}, u32[]{:S(2)}, u32[]{:S(2)}) collective-permute-start(bf16[4,96,256]{2,1,0:T(8,128)(2,1)S(1)} %get-tuple-element.40), channel_id=1, source_target_pairs={{0,4},{2,6},{4,0},{6,2},{8,12},{10,14},{12,8},{14,10},{16,20},{18,... | collective-permute-start | bytes 589832 | tf_op jit(solution)/shard_map/ppermute | solution.py:520
  103.9 9.9 %collective-permute-start.3 = (bf16[4,96,256]{2,1,0:T(8,128)(2,1)S(1)}, bf16[4,96,256]{2,1,0:T(8,128)(2,1)S(1)}, u32[]{:S(2)}, u32[]{:S(2)}) collective-permute-start(bf16[4,96,256]{2,1,0:T(8,128)(2,1)S(1)} %get-tuple-element.40), channel_id=1, source_target_pairs={{0,2},{2,0},{4,6},{6,4},{8,10},{10,8},{12,14},{14,12},{16,18},{18,... | collective-permute-start | bytes 589832 | tf_op jit(solution)/shard_map/ppermute | solution.py:520
  113.8 27.3 %all-to-all-start.3 = ((bf16[16,256,128]{2,1,0:T(8,128)(2,1)}), bf16[16,256,128]{2,1,0:T(8,128)(2,1)}, u32[]{:S(2)}, u32[]{:S(2)}) async-start(bf16[16,256,128]{2,1,0:T(8,128)(2,1)} %get-tuple-element.34), calls=%async_computation.3 | async-start | bytes 2097152 | tf_op jit(solution)/shard_map/all_to_all | solution.py:544
  119.8 4.5 %collective-permute-start.6 = (f32[32,64]{1,0:T(8,128)S(1)}, f32[32,64]{1,0:T(8,128)S(1)}, u32[]{:S(2)}, u32[]{:S(2)}) collective-permute-start(f32[32,64]{1,0:T(8,128)S(1)} %bitcast_reduce_fusion), channel_id=1, source_target_pairs={{0,1},{1,0},{2,3},{3,2},{4,5},{5,4},{6,7},{7,6},{8,9},{9,8},{10,11... | collective-permute-start | bytes 24584 | tf_op jit(solution)/shard_map/ppermute | solution.py:653

commit v4 on v3

--- a/solution.py
+++ b/solution.py
@@ -508,7 +508,7 @@
         + [wide] * (2 * len(factors))
         + [pltpu.SemaphoreType.DMA((copies,))],
         compiler_params=params(),
-        cost_estimate=estimate(rows * columns, rows * columns * (2 + 4 * len(factors))),
+        cost_estimate=estimate(1000, 1000),
     )(back, *factors)
 
 

time: 146 us -> 146 us (level)
  no operation moved by 1% of the time
where the time goes in v4:
time: 146 us; the launch traced here: 144 us
  Pallas kernels  53.1 us (36%)
  waiting for transfers between devices  39.6 us (27%)
  starting transfers between devices  33.6 us (23%)
  local copies, waits for them, and re-layouts  9.92 us (7%)
  other arithmetic  3.69 us (3%)
  matrix products  3.46 us (2%)
    all_to_all x4, starting transfers between devices, exchange(): lax.all_to_all(values, 'seq', split_axis=0, concat_axis=0, tiled=True)  25.7 us
    all_to_all x4, waiting for transfers between devices, exchange(): lax.all_to_all(values, 'seq', split_axis=0, concat_axis=0, tiled=True)  23 us
    pallas_call x1, Pallas kernels, per_device(): pl.pallas_call(grad_kernel, in_specs=[in_vmem, in_vmem, anywhere, anywher...  19.1 us
    ppermute x6, waiting for transfers between devices, swaps(): received.append(lax.ppermute(held, 'seq', pairs))  16.6 us
    pallas_call x1, Pallas kernels, per_device(): pl.pallas_call(conv_kernel, in_specs=[in_vmem, anywhere, in_vmem, in_vmem...  12.9 us
    pallas_call x1, Pallas kernels, per_device(): pl.pallas_call(filter_kernel, in_specs=[in_vmem] * 5, out_specs=[in_vmem,...  9.8 us
    ppermute x6, starting transfers between devices, swaps(): received.append(lax.ppermute(held, 'seq', pairs))  6.38 us
    pallas_call x2, Pallas kernels, ungate(): pl.pallas_call(functools.partial(ungate_kernel, group, len(factors)), in_...  5.81 us
  transfers between devices with their start and end apart: 11, of which 7 were waited for; matrix products, arithmetic and copies ran while one was open for 12% of the time, Pallas kernels for 33%

profile of v4, /device:TPU:0, one launch (start us, length us, event | category | flops | bytes accessed | tf_op | source)
XLA Modules:
  0.0 144.4 jit_solution(6333933635871658883)
XLA Ops:
  0.6 2.7 %shard_map.153 = bf16[16,256,128]{2,1,0:T(8,128)(2,1)} custom-call(bf16[128,4096]{1,0:T(8,128)(2,1)} %refs_2_.1, bf16[128,4096]{1,0:T(8,128)(2,1)} %refs_1_.3), custom_call_target="tpu_custom_call" | custom-call | flops 524288 | bytes 3145728 | tf_op jit(solution)/shard_map/pallas_call | solution.py:457
  3.4 7.4 %all-to-all-start = ((bf16[16,256,128]{2,1,0:T(8,128)(2,1)}), bf16[16,256,128]{2,1,0:T(8,128)(2,1)}, u32[]{:S(2)}, u32[]{:S(2)}) async-start(bf16[16,256,128]{2,1,0:T(8,128)(2,1)} %shard_map.153), calls=%async_computation | async-start | bytes 2097152 | tf_op jit(solution)/shard_map/all_to_all | solution.py:544
  10.8 0.8 fusion.13
  11.7 0.8 copy.25.w_t_ref
  12.5 0.8 dynamic_slice.10
  13.2 0.8 copy.26.decay_ref
  14.6 3.5 %cosine_bitcast_fusion = (f32[64,2048]{1,0:T(8,128)}, f32[64,2048]{1,0:T(8,128)}) fusion(f32[32,64]{1,0:T(8,128)S(1)} %copy-done, f32[16,2048]{1,0:T(8,128)S(1)} %get-tuple-element.44, f32[16,2048]{1,0:T(8,128)S(1)} %get-tuple-element.43), kind=kOutput, calls=%fused_computation.6 | convolution fusion | flops 50397184 | bytes 1318912 | tf_op jit(solution)/shard_map/dot_general | solution.py:552
  18.1 9.8 %shard_map.155 = (f32[256,2048]{1,0:T(8,128)}, f32[16,256,256]{2,1,0:T(8,128)}) custom-call(f32[256,64]{1,0:T(8,128)} %copy.25.w_t_ref, f32[64,2048]{1,0:T(8,128)} %get-tuple-element.38.hidden_ref, f32[256,1]{1,0:T(8,128)} %copy.26.decay_ref, f32[2,256,256]{2,1,0:T(8,128)} %constant.63.clone.table_ref, f32[16,256]{1,0:T(8,128)} %constant.64.clone.twiddle_ref), custom_call_target="tpu_custom_call" | custom-call | flops 1000 | bytes 1000 | tf_op jit(solution)/shard_map/pallas_call | solution.py:569
  27.9 0.8 dynamic_slice.11
  28.7 2.7 %shard_map.154 = bf16[16,256,128]{2,1,0:T(8,128)(2,1)} custom-call(bf16[128,4096]{1,0:T(8,128)(2,1)} %refs_1_.2, bf16[128,4096]{1,0:T(8,128)(2,1)} %right_any.3), custom_call_target="tpu_custom_call" | custom-call | flops 524288 | bytes 3145728 | tf_op jit(solution)/shard_map/pallas_call | solution.py:457
  31.4 1.5 %constant_dynamic-slice_fusion.w_ref = f32[64,256]{1,0:T(8,128)} fusion(f32[64,4096]{1,0:T(8,128)} %param.15, s32[]{:T(128)S(6)} %select_n.58), kind=kLoop, calls=%fused_computation.31 | loop fusion | bytes 131076 | tf_op jit(solution)/shard_map/dynamic_slice | solution.py:558
  33.8 6.9 %all-to-all-start.2 = ((bf16[16,256,128]{2,1,0:T(8,128)(2,1)}), bf16[16,256,128]{2,1,0:T(8,128)(2,1)}, u32[]{:S(2)}, u32[]{:S(2)}) async-start(bf16[16,256,128]{2,1,0:T(8,128)(2,1)} %shard_map.154), calls=%async_computation.2 | async-start | bytes 2097152 | tf_op jit(solution)/shard_map/all_to_all | solution.py:544
  40.8 0.8 copy.27.skip_ref
  41.6 12.9 %shard_map.156 = (bf16[16,256,128]{2,1,0:T(8,128)(2,1)}, f32[16,256,256]{2,1,0:T(8,128)}) custom-call(bf16[16,256,128]{2,1,0:T(8,128)(2,1)} %all-to-all-done.x_ref, f32[16,256,256]{2,1,0:T(8,128)} %get-tuple-element.24.h_any, f32[2,256,256]{2,1,0:T(8,128)} %constant.63.clone.table_ref, f32[16,256]{1,0:T(8,128)} %constant.64.clone.twiddle_ref, ...), custom_call_target="tpu_custom_call" | custom-call | flops 3221225472 | bytes 10485760 | tf_op jit(solution)/shard_map/pallas_call | solution.py:588
  54.5 9.3 %all-to-all-done.2.g_ref = bf16[16,256,128]{2,1,0:T(8,128)(2,1)} async-done(((bf16[16,256,128]{2,1,0:T(8,128)(2,1)}), bf16[16,256,128]{2,1,0:T(8,128)(2,1)}, u32[]{:S(2)}, u32[]{:S(2)}) %all-to-all-start.2) | async-done | bytes 1048608 | tf_op jit(solution)/shard_map/all_to_all | solution.py:544
  63.8 6.9 %all-to-all-start.1 = ((bf16[16,256,128]{2,1,0:T(8,128)(2,1)}), bf16[16,256,128]{2,1,0:T(8,128)(2,1)}, u32[]{:S(2)}, u32[]{:S(2)}) async-start(bf16[16,256,128]{2,1,0:T(8,128)(2,1)} %get-tuple-element.26), calls=%async_computation.1 | async-start | bytes 2097152 | tf_op jit(solution)/shard_map/all_to_all | solution.py:544
  70.7 19.1 %shard_map.158 = (bf16[16,256,128]{2,1,0:T(8,128)(2,1)}, bf16[96,256]{1,0:T(8,128)(2,1)}, bf16[64,64]{1,0:T(8,128)(2,1)}) custom-call(bf16[16,256,128]{2,1,0:T(8,128)(2,1)} %all-to-all-done.x_ref, bf16[16,256,128]{2,1,0:T(8,128)(2,1)} %all-to-all-done.2.g_ref, f32[16,256,256]{2,1,0:T(8,128)} %get-tuple-element.28.x_any, ...), custom_call_target="tpu_custom_call" | custom-call | flops 4831838208 | bytes 10485760 | tf_op jit(solution)/shard_map/pallas_call | solution.py:602
  89.9 3.7 %collective-permute-start.2 = (bf16[96,256]{1,0:T(8,128)(2,1)}, bf16[96,256]{1,0:T(8,128)(2,1)S(1)}, u32[]{:S(2)}, u32[]{:S(2)}) collective-permute-start(bf16[96,256]{1,0:T(8,128)(2,1)} %get-tuple-element.33), channel_id=1, source_target_pairs={{0,24},{2,26},{4,28},{6,30},{8,16},{10,18},{12,20},{14,22},{16,8},... | collective-permute-start | bytes 147464 | tf_op jit(solution)/shard_map/ppermute | solution.py:520
  93.6 0.7 collective-permute-start
  94.3 1.8 %collective-permute-done.2 = bf16[96,256]{1,0:T(8,128)(2,1)S(1)} collective-permute-done((bf16[96,256]{1,0:T(8,128)(2,1)}, bf16[96,256]{1,0:T(8,128)(2,1)S(1)}, u32[]{:S(2)}, u32[]{:S(2)}) %collective-permute-start.2) | collective-permute-done | bytes 49184 | tf_op jit(solution)/shard_map/ppermute | solution.py:520
  96.1 5.3 %collective-permute-done.1 = bf16[96,256]{1,0:T(8,128)(2,1)S(1)} collective-permute-done((bf16[96,256]{1,0:T(8,128)(2,1)}, bf16[96,256]{1,0:T(8,128)(2,1)S(1)}, u32[]{:S(2)}, u32[]{:S(2)}) %collective-permute-start.1) | collective-permute-done | bytes 49184 | tf_op jit(solution)/shard_map/ppermute | solution.py:520
  101.4 0.8 fusion.11
  102.2 0.8 collective-permute-start.5
  103.0 0.8 collective-permute-start.4
  104.2 5.3 %collective-permute-done.5 = bf16[4,96,256]{2,1,0:T(8,128)(2,1)S(1)} collective-permute-done((bf16[4,96,256]{2,1,0:T(8,128)(2,1)S(1)}, bf16[4,96,256]{2,1,0:T(8,128)(2,1)S(1)}, u32[]{:S(2)}, u32[]{:S(2)}) %collective-permute-start.5) | collective-permute-done | bytes 196640 | tf_op jit(solution)/shard_map/ppermute | solution.py:520
  109.5 4.3 %collective-permute-done.4 = bf16[4,96,256]{2,1,0:T(8,128)(2,1)S(1)} collective-permute-done((bf16[4,96,256]{2,1,0:T(8,128)(2,1)S(1)}, bf16[4,96,256]{2,1,0:T(8,128)(2,1)S(1)}, u32[]{:S(2)}, u32[]{:S(2)}) %collective-permute-start.4) | collective-permute-done | bytes 196640 | tf_op jit(solution)/shard_map/ppermute | solution.py:520
  113.8 4.4 %all-to-all-start.3 = ((bf16[16,256,128]{2,1,0:T(8,128)(2,1)}), bf16[16,256,128]{2,1,0:T(8,128)(2,1)}, u32[]{:S(2)}, u32[]{:S(2)}) async-start(bf16[16,256,128]{2,1,0:T(8,128)(2,1)} %get-tuple-element.34), calls=%async_computation.3 | async-start | bytes 2097152 | tf_op jit(solution)/shard_map/all_to_all | solution.py:544
  119.8 1.6 %collective-permute-start.6 = (f32[32,64]{1,0:T(8,128)S(1)}, f32[32,64]{1,0:T(8,128)S(1)}, u32[]{:S(2)}, u32[]{:S(2)}) collective-permute-start(f32[32,64]{1,0:T(8,128)S(1)} %bitcast_reduce_fusion), channel_id=1, source_target_pairs={{0,1},{1,0},{2,3},{3,2},{4,5},{5,4},{6,7},{7,6},{8,9},{9,8},{10,11... | collective-permute-start | bytes 24584 | tf_op jit(solution)/shard_map/ppermute | solution.py:653
  121.6 1.6 %copy.32 = f32[8,8,16,256]{3,1,2,0:T(8,128)} copy(f32[8,8,16,256]{3,2,1,0:T(8,128)S(1)} %bitcast.39) | data formatting | bytes 2097152
  125.0 2.7 %shard_map.157 = bf16[128,4096]{1,0:T(8,128)(2,1)} custom-call(bf16[16,256,128]{2,1,0:T(8,128)(2,1)} %all-to-all-done.1.refs_0_, bf16[128,4096]{1,0:T(8,128)(2,1)} %refs_1_.2), custom_call_target="tpu_custom_call" | custom-call | flops 1000 | bytes 1000 | tf_op jit(solution)/shard_map/pallas_call | solution.py:502
  127.7 13.4 %all-to-all-done.3.refs_0_ = bf16[16,256,128]{2,1,0:T(8,128)(2,1)} async-done(((bf16[16,256,128]{2,1,0:T(8,128)(2,1)}), bf16[16,256,128]{2,1,0:T(8,128)(2,1)}, u32[]{:S(2)}, u32[]{:S(2)}) %all-to-all-start.3) | async-done | bytes 1048608 | tf_op jit(solution)/shard_map/all_to_all | solution.py:544
  141.1 3.1 %shard_map.159 = (bf16[128,4096]{1,0:T(8,128)(2,1)}, bf16[128,4096]{1,0:T(8,128)(2,1)}) custom-call(bf16[16,256,128]{2,1,0:T(8,128)(2,1)} %all-to-all-done.3.refs_0_, bf16[128,4096]{1,0:T(8,128)(2,1)} %refs_1_.3, bf16[128,4096]{1,0:T(8,128)(2,1)} %refs_2_.1), custom_call_target="tpu_custom_call" | custom-call | flops 1000 | bytes 1000 | tf_op jit(solution)/shard_map/pallas_call | solution.py:502
  (29 shorter events, 5.5 us)
Async XLA Ops:
  0.6 14.0 %copy-start = (f32[32,64]{1,0:T(8,128)S(1)}, f32[32,64]{1,0:T(8,128)}, u32[]{:S(2)}) copy-start(f32[32,64]{1,0:T(8,128)} %param.14) | copy-start | bytes 24580
  3.4 30.5 %all-to-all-start = ((bf16[16,256,128]{2,1,0:T(8,128)(2,1)}), bf16[16,256,128]{2,1,0:T(8,128)(2,1)}, u32[]{:S(2)}, u32[]{:S(2)}) async-start(bf16[16,256,128]{2,1,0:T(8,128)(2,1)} %shard_map.153), calls=%async_computation | async-start | bytes 2097152 | tf_op jit(solution)/shard_map/all_to_all | solution.py:544
  33.8 29.9 %all-to-all-start.2 = ((bf16[16,256,128]{2,1,0:T(8,128)(2,1)}), bf16[16,256,128]{2,1,0:T(8,128)(2,1)}, u32[]{:S(2)}, u32[]{:S(2)}) async-start(bf16[16,256,128]{2,1,0:T(8,128)(2,1)} %shard_map.154), calls=%async_computation.2 | async-start | bytes 2097152 | tf_op jit(solution)/shard_map/all_to_all | solution.py:544
  63.8 50.1 %all-to-all-start.1 = ((bf16[16,256,128]{2,1,0:T(8,128)(2,1)}), bf16[16,256,128]{2,1,0:T(8,128)(2,1)}, u32[]{:S(2)}, u32[]{:S(2)}) async-start(bf16[16,256,128]{2,1,0:T(8,128)(2,1)} %get-tuple-element.26), calls=%async_computation.1 | async-start | bytes 2097152 | tf_op jit(solution)/shard_map/all_to_all | solution.py:544
  89.9 6.2 %collective-permute-start.2 = (bf16[96,256]{1,0:T(8,128)(2,1)}, bf16[96,256]{1,0:T(8,128)(2,1)S(1)}, u32[]{:S(2)}, u32[]{:S(2)}) collective-permute-start(bf16[96,256]{1,0:T(8,128)(2,1)} %get-tuple-element.33), channel_id=1, source_target_pairs={{0,24},{2,26},{4,28},{6,30},{8,16},{10,18},{12,20},{14,22},{16,8},... | collective-permute-start | bytes 147464 | tf_op jit(solution)/shard_map/ppermute | solution.py:520
  93.6 7.8 %collective-permute-start.1 = (bf16[96,256]{1,0:T(8,128)(2,1)}, bf16[96,256]{1,0:T(8,128)(2,1)S(1)}, u32[]{:S(2)}, u32[]{:S(2)}) collective-permute-start(bf16[96,256]{1,0:T(8,128)(2,1)} %get-tuple-element.33), channel_id=1, source_target_pairs={{0,16},{2,18},{4,20},{6,22},{8,24},{10,26},{12,28},{14,30},{16,0},... | collective-permute-start | bytes 147464 | tf_op jit(solution)/shard_map/ppermute | solution.py:520
  93.6 7.8 %collective-permute-start = (bf16[96,256]{1,0:T(8,128)(2,1)}, bf16[96,256]{1,0:T(8,128)(2,1)S(1)}, u32[]{:S(2)}, u32[]{:S(2)}) collective-permute-start(bf16[96,256]{1,0:T(8,128)(2,1)} %get-tuple-element.33), channel_id=1, source_target_pairs={{0,8},{2,10},{4,12},{6,14},{8,0},{10,2},{12,4},{14,6},{16,24},{18,... | collective-permute-start | bytes 147464 | tf_op jit(solution)/shard_map/ppermute | solution.py:520
  102.2 7.2 %collective-permute-start.5 = (bf16[4,96,256]{2,1,0:T(8,128)(2,1)S(1)}, bf16[4,96,256]{2,1,0:T(8,128)(2,1)S(1)}, u32[]{:S(2)}, u32[]{:S(2)}) collective-permute-start(bf16[4,96,256]{2,1,0:T(8,128)(2,1)S(1)} %get-tuple-element.40), channel_id=1, source_target_pairs={{0,6},{2,4},{4,2},{6,0},{8,14},{10,12},{12,10},{14,8},{16,22},{18,... | collective-permute-start | bytes 589832 | tf_op jit(solution)/shard_map/ppermute | solution.py:520
  103.0 10.7 %collective-permute-start.4 = (bf16[4,96,256]{2,1,0:T(8,128)(2,1)S(1)}, bf16[4,96,256]{2,1,0:T(8,128)(2,1)S(1)}, u32[]{:S(2)}, u32[]{:S(2)}) collective-permute-start(bf16[4,96,256]{2,1,0:T(8,128)(2,1)S(1)} %get-tuple-element.40), channel_id=1, source_target_pairs={{0,4},{2,6},{4,0},{6,2},{8,12},{10,14},{12,8},{14,10},{16,20},{18,... | collective-permute-start | bytes 589832 | tf_op jit(solution)/shard_map/ppermute | solution.py:520
  103.9 9.9 %collective-permute-start.3 = (bf16[4,96,256]{2,1,0:T(8,128)(2,1)S(1)}, bf16[4,96,256]{2,1,0:T(8,128)(2,1)S(1)}, u32[]{:S(2)}, u32[]{:S(2)}) collective-permute-start(bf16[4,96,256]{2,1,0:T(8,128)(2,1)S(1)} %get-tuple-element.40), channel_id=1, source_target_pairs={{0,2},{2,0},{4,6},{6,4},{8,10},{10,8},{12,14},{14,12},{16,18},{18,... | collective-permute-start | bytes 589832 | tf_op jit(solution)/shard_map/ppermute | solution.py:520
  113.8 27.3 %all-to-all-start.3 = ((bf16[16,256,128]{2,1,0:T(8,128)(2,1)}), bf16[16,256,128]{2,1,0:T(8,128)(2,1)}, u32[]{:S(2)}, u32[]{:S(2)}) async-start(bf16[16,256,128]{2,1,0:T(8,128)(2,1)} %get-tuple-element.34), calls=%async_computation.3 | async-start | bytes 2097152 | tf_op jit(solution)/shard_map/all_to_all | solution.py:544
  119.8 4.5 %collective-permute-start.6 = (f32[32,64]{1,0:T(8,128)S(1)}, f32[32,64]{1,0:T(8,128)S(1)}, u32[]{:S(2)}, u32[]{:S(2)}) collective-permute-start(f32[32,64]{1,0:T(8,128)S(1)} %bitcast_reduce_fusion), channel_id=1, source_target_pairs={{0,1},{1,0},{2,3},{3,2},{4,5},{5,4},{6,7},{7,6},{8,9},{9,8},{10,11... | collective-permute-start | bytes 24584 | tf_op jit(solution)/shard_map/ppermute | solution.py:653

commit v5 on v2

--- a/solution.py
+++ b/solution.py
@@ -378,7 +378,7 @@
     small_ref[hidden_count:, :] = tail.astype(jnp.bfloat16)
 
 
-def params(limit=56):
+def params(limit=63):
     return pltpu.CompilerParams(vmem_limit_bytes=limit * MIB)
 
 

time: 138 us -> 136 us (0.986)
  other arithmetic: 7.3 us -> 2.89 us
  waiting for transfers between devices: 25.8 us -> 28.6 us
    all_to_all x4, waiting for transfers between devices: 11.5 us -> 15.6 us  [exchange(): lax.all_to_all(values, 'seq', split_axis=0, concat_axis=0, tiled=True)]
    unnamed x16 -> x6, local copies, waits for them, and re-layouts: 5.57 us -> 3.59 us
    another operation x2, other arithmetic: 1.83 us -> 0.14 us  [swaps(): return jnp.stack(received)]
  transfers between devices with their start and end apart: 11 -> 11, of which waited for: 7 -> 7; matrix products, arithmetic and copies ran while one was open for 16% -> 13% of each run, Pallas kernels for 35% -> 35%
where the time goes in v5:
time: 136 us; the launch traced here: 134 us
  Pallas kernels  53 us (39%)
  starting transfers between devices  33.5 us (25%)
  waiting for transfers between devices  28.6 us (21%)
  local copies, waits for them, and re-layouts  11.5 us (8%)
  matrix products  3.46 us (3%)
  other arithmetic  2.89 us (2%)
    all_to_all x4, starting transfers between devices, exchange(): lax.all_to_all(values, 'seq', split_axis=0, concat_axis=0, tiled=True)  25.6 us
    pallas_call x1, Pallas kernels, per_device(): pl.pallas_call(grad_kernel, in_specs=[in_vmem, in_vmem, anywhere, anywher...  19 us
    all_to_all x4, waiting for transfers between devices, exchange(): lax.all_to_all(values, 'seq', split_axis=0, concat_axis=0, tiled=True)  15.6 us
    ppermute x6, waiting for transfers between devices, swaps(): received.append(lax.ppermute(held, 'seq', pairs))  13 us
    pallas_call x1, Pallas kernels, per_device(): pl.pallas_call(conv_kernel, in_specs=[in_vmem, anywhere, in_vmem, in_vmem...  12.9 us
    pallas_call x1, Pallas kernels, per_device(): pl.pallas_call(filter_kernel, in_specs=[in_vmem] * 5, out_specs=[in_vmem,...  9.8 us
    ppermute x6, starting transfers between devices, swaps(): received.append(lax.ppermute(held, 'seq', pairs))  6.31 us
    pallas_call x2, Pallas kernels, ungate(): pl.pallas_call(functools.partial(ungate_kernel, group, len(factors)), in_...  5.81 us
  transfers between devices with their start and end apart: 11, of which 7 were waited for; matrix products, arithmetic and copies ran while one was open for 13% of the time, Pallas kernels for 35%

profile of v5, /device:TPU:0, one launch (start us, length us, event | category | flops | bytes accessed | tf_op | source)
XLA Modules:
  0.0 133.9 jit_solution(6956899499325249434)
XLA Ops:
  0.6 2.7 %shard_map.153 = bf16[16,256,128]{2,1,0:T(8,128)(2,1)} custom-call(bf16[128,4096]{1,0:T(8,128)(2,1)} %refs_2_.1, bf16[128,4096]{1,0:T(8,128)(2,1)} %refs_1_.3), custom_call_target="tpu_custom_call" | custom-call | flops 524288 | bytes 3145728 | tf_op jit(solution)/shard_map/pallas_call | solution.py:451
  3.4 7.4 %all-to-all-start = ((bf16[16,256,128]{2,1,0:T(8,128)(2,1)}), bf16[16,256,128]{2,1,0:T(8,128)(2,1)}, u32[]{:S(2)}, u32[]{:S(2)}) async-start(bf16[16,256,128]{2,1,0:T(8,128)(2,1)} %shard_map.153), calls=%async_computation | async-start | bytes 2097152 | tf_op jit(solution)/shard_map/all_to_all | solution.py:538
  10.8 0.8 fusion.13
  11.7 0.8 copy.25.w_t_ref
  12.5 0.8 dynamic_slice.10
  13.2 0.8 copy.26.decay_ref
  14.6 3.5 %cosine_bitcast_fusion = (f32[64,2048]{1,0:T(8,128)}, f32[64,2048]{1,0:T(8,128)}) fusion(f32[32,64]{1,0:T(8,128)S(1)} %copy-done, f32[16,2048]{1,0:T(8,128)S(1)} %get-tuple-element.46, f32[16,2048]{1,0:T(8,128)S(1)} %get-tuple-element.45), kind=kOutput, calls=%fused_computation.6 | convolution fusion | flops 50397184 | bytes 1318912 | tf_op jit(solution)/shard_map/dot_general | solution.py:546
  18.1 9.8 %shard_map.155 = (f32[256,2048]{1,0:T(8,128)}, f32[16,256,256]{2,1,0:T(8,128)}) custom-call(f32[256,64]{1,0:T(8,128)} %copy.25.w_t_ref, f32[64,2048]{1,0:T(8,128)} %get-tuple-element.40.hidden_ref, f32[256,1]{1,0:T(8,128)} %copy.26.decay_ref, f32[2,256,256]{2,1,0:T(8,128)} %constant.63.clone.table_ref, f32[16,256]{1,0:T(8,128)} %constant.64.clone.twiddle_ref), custom_call_target="tpu_custom_call" | custom-call | flops 1000 | bytes 1000 | tf_op jit(solution)/shard_map/pallas_call | solution.py:563
  27.9 0.8 dynamic_slice.11
  28.7 2.7 %shard_map.154 = bf16[16,256,128]{2,1,0:T(8,128)(2,1)} custom-call(bf16[128,4096]{1,0:T(8,128)(2,1)} %refs_1_.2, bf16[128,4096]{1,0:T(8,128)(2,1)} %right_any.3), custom_call_target="tpu_custom_call" | custom-call | flops 524288 | bytes 3145728 | tf_op jit(solution)/shard_map/pallas_call | solution.py:451
  31.4 1.5 %constant_dynamic-slice_fusion.w_ref = f32[64,256]{1,0:T(8,128)} fusion(f32[64,4096]{1,0:T(8,128)} %param.15, s32[]{:T(128)S(6)} %select_n.58), kind=kLoop, calls=%fused_computation.32 | loop fusion | bytes 131076 | tf_op jit(solution)/shard_map/dynamic_slice | solution.py:552
  33.8 6.9 %all-to-all-start.2 = ((bf16[16,256,128]{2,1,0:T(8,128)(2,1)}), bf16[16,256,128]{2,1,0:T(8,128)(2,1)}, u32[]{:S(2)}, u32[]{:S(2)}) async-start(bf16[16,256,128]{2,1,0:T(8,128)(2,1)} %shard_map.154), calls=%async_computation.2 | async-start | bytes 2097152 | tf_op jit(solution)/shard_map/all_to_all | solution.py:538
  40.8 0.8 copy.27.skip_ref
  41.6 12.9 %shard_map.156 = (bf16[16,256,128]{2,1,0:T(8,128)(2,1)}, f32[16,256,256]{2,1,0:T(8,128)}) custom-call(bf16[16,256,128]{2,1,0:T(8,128)(2,1)} %all-to-all-done.x_ref, f32[16,256,256]{2,1,0:T(8,128)} %get-tuple-element.25.h_any, f32[2,256,256]{2,1,0:T(8,128)} %constant.63.clone.table_ref, f32[16,256]{1,0:T(8,128)} %constant.64.clone.twiddle_ref, ...), custom_call_target="tpu_custom_call" | custom-call | flops 3221225472 | bytes 10485760 | tf_op jit(solution)/shard_map/pallas_call | solution.py:582
  54.5 9.3 %all-to-all-done.2.g_ref = bf16[16,256,128]{2,1,0:T(8,128)(2,1)} async-done(((bf16[16,256,128]{2,1,0:T(8,128)(2,1)}), bf16[16,256,128]{2,1,0:T(8,128)(2,1)}, u32[]{:S(2)}, u32[]{:S(2)}) %all-to-all-start.2) | async-done | bytes 1048608 | tf_op jit(solution)/shard_map/all_to_all | solution.py:538
  63.8 6.9 %all-to-all-start.1 = ((bf16[16,256,128]{2,1,0:T(8,128)(2,1)}), bf16[16,256,128]{2,1,0:T(8,128)(2,1)}, u32[]{:S(2)}, u32[]{:S(2)}) async-start(bf16[16,256,128]{2,1,0:T(8,128)(2,1)} %get-tuple-element.27), calls=%async_computation.1 | async-start | bytes 2097152 | tf_op jit(solution)/shard_map/all_to_all | solution.py:538
  70.7 19.0 %shard_map.158 = (bf16[16,256,128]{2,1,0:T(8,128)(2,1)}, bf16[80,256]{1,0:T(8,128)(2,1)}, bf16[64,64]{1,0:T(8,128)(2,1)}) custom-call(bf16[16,256,128]{2,1,0:T(8,128)(2,1)} %all-to-all-done.x_ref, bf16[16,256,128]{2,1,0:T(8,128)(2,1)} %all-to-all-done.2.g_ref, f32[16,256,256]{2,1,0:T(8,128)} %get-tuple-element.29.x_any, ...), custom_call_target="tpu_custom_call" | custom-call | flops 4831838208 | bytes 10485760 | tf_op jit(solution)/shard_map/pallas_call | solution.py:593
  89.7 0.8 reshape.51
  90.5 0.8 constant_dynamic-update-slice_fusion.1
  91.3 3.7 %collective-permute-start.2 = (bf16[96,256]{1,0:T(8,128)(2,1)S(1)}, bf16[96,256]{1,0:T(8,128)(2,1)S(1)}, u32[]{:S(2)}, u32[]{:S(2)}) collective-permute-start(bf16[96,256]{1,0:T(8,128)(2,1)S(1)} %constant_dynamic-update-slice_fusion), channel_id=1, source_target_pairs={{0,24},{2,26},{4,28},{6,30},{8,16},{10,18},{12,20},{14,22},{16,8},... | collective-permute-start | bytes 147464 | tf_op jit(solution)/shard_map/ppermute | solution.py:514
  95.7 1.5 %collective-permute-done.2 = bf16[96,256]{1,0:T(8,128)(2,1)S(1)} collective-permute-done((bf16[96,256]{1,0:T(8,128)(2,1)S(1)}, bf16[96,256]{1,0:T(8,128)(2,1)S(1)}, u32[]{:S(2)}, u32[]{:S(2)}) %collective-permute-start.2) | collective-permute-done | bytes 49184 | tf_op jit(solution)/shard_map/ppermute | solution.py:514
  97.2 4.2 %collective-permute-done.1 = bf16[96,256]{1,0:T(8,128)(2,1)S(1)} collective-permute-done((bf16[96,256]{1,0:T(8,128)(2,1)S(1)}, bf16[96,256]{1,0:T(8,128)(2,1)S(1)}, u32[]{:S(2)}, u32[]{:S(2)}) %collective-permute-start.1) | collective-permute-done | bytes 49184 | tf_op jit(solution)/shard_map/ppermute | solution.py:514
  101.4 0.8 collective-permute-start.5
  102.2 0.8 collective-permute-start.4
  103.4 4.4 %all-to-all-start.3 = ((bf16[16,256,128]{2,1,0:T(8,128)(2,1)}), bf16[16,256,128]{2,1,0:T(8,128)(2,1)}, u32[]{:S(2)}, u32[]{:S(2)}) async-start(bf16[16,256,128]{2,1,0:T(8,128)(2,1)} %get-tuple-element.36), calls=%async_computation.3 | async-start | bytes 2097152 | tf_op jit(solution)/shard_map/all_to_all | solution.py:538
  107.7 0.9 collective-permute-done.5
  108.7 6.3 %collective-permute-done.4 = bf16[4,96,256]{2,1,0:T(8,128)(2,1)S(1)} collective-permute-done((bf16[4,96,256]{2,1,0:T(8,128)(2,1)S(1)}, bf16[4,96,256]{2,1,0:T(8,128)(2,1)S(1)}, u32[]{:S(2)}, u32[]{:S(2)}) %collective-permute-start.4) | collective-permute-done | bytes 196640 | tf_op jit(solution)/shard_map/ppermute | solution.py:514
  116.7 1.6 %collective-permute-start.6 = (f32[32,64]{1,0:T(8,128)S(1)}, f32[32,64]{1,0:T(8,128)S(1)}, u32[]{:S(2)}, u32[]{:S(2)}) collective-permute-start(f32[32,64]{1,0:T(8,128)S(1)} %reduce_sum.19), channel_id=1, source_target_pairs={{0,1},{1,0},{2,3},{3,2},{4,5},{5,4},{6,7},{7,6},{8,9},{9,8},{10,11... | collective-permute-start | bytes 24584 | tf_op jit(solution)/shard_map/ppermute | solution.py:640
  118.4 1.6 %copy.31 = f32[8,8,16,256]{3,1,2,0:T(8,128)} copy(f32[8,8,16,256]{3,2,1,0:T(8,128)S(1)} %bitcast.35) | data formatting | bytes 2097152
  121.8 2.7 %shard_map.157 = bf16[128,4096]{1,0:T(8,128)(2,1)} custom-call(bf16[16,256,128]{2,1,0:T(8,128)(2,1)} %all-to-all-done.1.refs_0_, bf16[128,4096]{1,0:T(8,128)(2,1)} %refs_1_.2), custom_call_target="tpu_custom_call" | custom-call | flops 524288 | bytes 3145728 | tf_op jit(solution)/shard_map/pallas_call | solution.py:496
  124.6 6.1 %all-to-all-done.3.refs_0_ = bf16[16,256,128]{2,1,0:T(8,128)(2,1)} async-done(((bf16[16,256,128]{2,1,0:T(8,128)(2,1)}), bf16[16,256,128]{2,1,0:T(8,128)(2,1)}, u32[]{:S(2)}, u32[]{:S(2)}) %all-to-all-start.3) | async-done | bytes 1048608 | tf_op jit(solution)/shard_map/all_to_all | solution.py:538
  130.7 3.1 %shard_map.159 = (bf16[128,4096]{1,0:T(8,128)(2,1)}, bf16[128,4096]{1,0:T(8,128)(2,1)}) custom-call(bf16[16,256,128]{2,1,0:T(8,128)(2,1)} %all-to-all-done.3.refs_0_, bf16[128,4096]{1,0:T(8,128)(2,1)} %refs_1_.3, bf16[128,4096]{1,0:T(8,128)(2,1)} %refs_2_.1), custom_call_target="tpu_custom_call" | custom-call | flops 524288 | bytes 5242880 | tf_op jit(solution)/shard_map/pallas_call | solution.py:496
  (31 shorter events, 6.3 us)
Async XLA Ops:
  0.6 14.0 %copy-start = (f32[32,64]{1,0:T(8,128)S(1)}, f32[32,64]{1,0:T(8,128)}, u32[]{:S(2)}) copy-start(f32[32,64]{1,0:T(8,128)} %param.14) | copy-start | bytes 24580
  3.4 30.5 %all-to-all-start = ((bf16[16,256,128]{2,1,0:T(8,128)(2,1)}), bf16[16,256,128]{2,1,0:T(8,128)(2,1)}, u32[]{:S(2)}, u32[]{:S(2)}) async-start(bf16[16,256,128]{2,1,0:T(8,128)(2,1)} %shard_map.153), calls=%async_computation | async-start | bytes 2097152 | tf_op jit(solution)/shard_map/all_to_all | solution.py:538
  33.8 29.9 %all-to-all-start.2 = ((bf16[16,256,128]{2,1,0:T(8,128)(2,1)}), bf16[16,256,128]{2,1,0:T(8,128)(2,1)}, u32[]{:S(2)}, u32[]{:S(2)}) async-start(bf16[16,256,128]{2,1,0:T(8,128)(2,1)} %shard_map.154), calls=%async_computation.2 | async-start | bytes 2097152 | tf_op jit(solution)/shard_map/all_to_all | solution.py:538
  63.8 39.6 %all-to-all-start.1 = ((bf16[16,256,128]{2,1,0:T(8,128)(2,1)}), bf16[16,256,128]{2,1,0:T(8,128)(2,1)}, u32[]{:S(2)}, u32[]{:S(2)}) async-start(bf16[16,256,128]{2,1,0:T(8,128)(2,1)} %get-tuple-element.27), calls=%async_computation.1 | async-start | bytes 2097152 | tf_op jit(solution)/shard_map/all_to_all | solution.py:538
  91.3 5.9 %collective-permute-start.2 = (bf16[96,256]{1,0:T(8,128)(2,1)S(1)}, bf16[96,256]{1,0:T(8,128)(2,1)S(1)}, u32[]{:S(2)}, u32[]{:S(2)}) collective-permute-start(bf16[96,256]{1,0:T(8,128)(2,1)S(1)} %constant_dynamic-update-slice_fusion), channel_id=1, source_target_pairs={{0,24},{2,26},{4,28},{6,30},{8,16},{10,18},{12,20},{14,22},{16,8},... | collective-permute-start | bytes 147464 | tf_op jit(solution)/shard_map/ppermute | solution.py:514
  95.0 6.4 %collective-permute-start.1 = (bf16[96,256]{1,0:T(8,128)(2,1)S(1)}, bf16[96,256]{1,0:T(8,128)(2,1)S(1)}, u32[]{:S(2)}, u32[]{:S(2)}) collective-permute-start(bf16[96,256]{1,0:T(8,128)(2,1)S(1)} %constant_dynamic-update-slice_fusion), channel_id=1, source_target_pairs={{0,16},{2,18},{4,20},{6,22},{8,24},{10,26},{12,28},{14,30},{16,0},... | collective-permute-start | bytes 147464 | tf_op jit(solution)/shard_map/ppermute | solution.py:514
  95.0 6.4 %collective-permute-start = (bf16[96,256]{1,0:T(8,128)(2,1)S(1)}, bf16[96,256]{1,0:T(8,128)(2,1)S(1)}, u32[]{:S(2)}, u32[]{:S(2)}) collective-permute-start(bf16[96,256]{1,0:T(8,128)(2,1)S(1)} %constant_dynamic-update-slice_fusion), channel_id=1, source_target_pairs={{0,8},{2,10},{4,12},{6,14},{8,0},{10,2},{12,4},{14,6},{16,24},{18,... | collective-permute-start | bytes 147464 | tf_op jit(solution)/shard_map/ppermute | solution.py:514
  101.4 7.2 %collective-permute-start.5 = (bf16[4,96,256]{2,1,0:T(8,128)(2,1)S(1)}, bf16[4,96,256]{2,1,0:T(8,128)(2,1)S(1)}, u32[]{:S(2)}, u32[]{:S(2)}) collective-permute-start(bf16[4,96,256]{2,1,0:T(8,128)(2,1)S(1)} %get-tuple-element.42), channel_id=1, source_target_pairs={{0,6},{2,4},{4,2},{6,0},{8,14},{10,12},{12,10},{14,8},{16,22},{18,... | collective-permute-start | bytes 589832 | tf_op jit(solution)/shard_map/ppermute | solution.py:514
  102.2 12.8 %collective-permute-start.4 = (bf16[4,96,256]{2,1,0:T(8,128)(2,1)S(1)}, bf16[4,96,256]{2,1,0:T(8,128)(2,1)S(1)}, u32[]{:S(2)}, u32[]{:S(2)}) collective-permute-start(bf16[4,96,256]{2,1,0:T(8,128)(2,1)S(1)} %get-tuple-element.42), channel_id=1, source_target_pairs={{0,4},{2,6},{4,0},{6,2},{8,12},{10,14},{12,8},{14,10},{16,20},{18,... | collective-permute-start | bytes 589832 | tf_op jit(solution)/shard_map/ppermute | solution.py:514
  103.1 11.9 %collective-permute-start.3 = (bf16[4,96,256]{2,1,0:T(8,128)(2,1)S(1)}, bf16[4,96,256]{2,1,0:T(8,128)(2,1)S(1)}, u32[]{:S(2)}, u32[]{:S(2)}) collective-permute-start(bf16[4,96,256]{2,1,0:T(8,128)(2,1)S(1)} %get-tuple-element.42), channel_id=1, source_target_pairs={{0,2},{2,0},{4,6},{6,4},{8,10},{10,8},{12,14},{14,12},{16,18},{18,... | collective-permute-start | bytes 589832 | tf_op jit(solution)/shard_map/ppermute | solution.py:514
  103.4 27.3 %all-to-all-start.3 = ((bf16[16,256,128]{2,1,0:T(8,128)(2,1)}), bf16[16,256,128]{2,1,0:T(8,128)(2,1)}, u32[]{:S(2)}, u32[]{:S(2)}) async-start(bf16[16,256,128]{2,1,0:T(8,128)(2,1)} %get-tuple-element.36), calls=%async_computation.3 | async-start | bytes 2097152 | tf_op jit(solution)/shard_map/all_to_all | solution.py:538
  116.7 4.5 %collective-permute-start.6 = (f32[32,64]{1,0:T(8,128)S(1)}, f32[32,64]{1,0:T(8,128)S(1)}, u32[]{:S(2)}, u32[]{:S(2)}) collective-permute-start(f32[32,64]{1,0:T(8,128)S(1)} %reduce_sum.19), channel_id=1, source_target_pairs={{0,1},{1,0},{2,3},{3,2},{4,5},{5,4},{6,7},{7,6},{8,9},{9,8},{10,11... | collective-permute-start | bytes 24584 | tf_op jit(solution)/shard_map/ppermute | solution.py:640
